TPU v7x, 32 devices: a whole 2x2x4 slice. The times are simulated.
32 devices in a mesh: dp: 4 (over y, x), expert: 8 (over z, core).
Axes of the slice: x: 2, y: 2, z: 4, core: 2. Of those that a mesh axis runs over, the one named last changes fastest.
Arguments:
- tokens: bfloat16 [4096, 2048], P(('dp', 'expert')), may hold values from -6 to 6
- cotangent: bfloat16 [4096, 2048], P(('dp', 'expert')), may hold values from -6 to 6
- expert_ids: int32 [4096, 2], P(('dp', 'expert')), may hold values from 0 to 7, all different within a row; in each aligned block of 128 rows (0 to 127, 128 to 255, ...) at most 40 rows name the same one
- gate_prob: float32 [4096, 2], P(('dp', 'expert')), may hold values from 0.2 to 1
- gate_weight: bfloat16 [8, 2048, 1408], P(None, 'expert', 'dp'), may hold values from -0.125 to 0.125
- up_weight: bfloat16 [8, 2048, 1408], P(None, 'expert', 'dp'), may hold values from -0.125 to 0.125
- down_weight: bfloat16 [8, 2048, 1408], P(None, 'expert', 'dp'), may hold values from -0.15625 to 0.15625
Outputs:
- mixed_out: bfloat16 [4096, 2048], P(('dp', 'expert'))
- grad_tokens: bfloat16 [4096, 2048], P(('dp', 'expert'))
- grad_gate: bfloat16 [8, 2048, 1408], P(None, 'expert', 'dp')
- grad_up: bfloat16 [8, 2048, 1408], P(None, 'expert', 'dp')
- grad_down: bfloat16 [8, 2048, 1408], P(None, 'expert', 'dp')
Inputs may be any that keep to these rules, and one draw needn't show every extreme that they name: `expert_ids`: among the 128 rows of one device no expert is named by more than 40 pairs, and in some device's rows one expert is named by exactly 40.
All inputs are finite; a program needn't handle non-finite values.
Results may differ from a plain program's by a relative error of at most 0.011.
Values may be sent and summed in bfloat16 or wider, within the bound.
A program may use at most 192 MiB of HBM per device.

v0:
```python
import jax
import jax.numpy as jnp
from jax import lax
from jax.sharding import PartitionSpec as P

TOPK = 2
BLOCK = 128


def shortened(array):

    def short(part):
        return part.astype(jnp.bfloat16) if part.dtype == jnp.float32 else part

    return jax.tree.map(short, array)


def slot_index(expert_ids, experts, capacity):
    flat_ids = expert_ids.reshape(-1)
    one_hot = (flat_ids[:, None] == jnp.arange(experts, dtype=jnp.int32)[None, :]).astype(jnp.int32)
    before = jnp.cumsum(one_hot, axis=0) - one_hot
    return flat_ids * capacity + jnp.sum(before * one_hot, axis=1)


def packing(flags):
    is_valid = flags.reshape(-1)
    is_empty = 1 - is_valid
    filled = jnp.sum(is_valid)
    target = jnp.where(
        is_valid == 1, jnp.cumsum(is_valid) - is_valid, filled + jnp.cumsum(is_empty) - is_empty
    )
    return (target.astype(jnp.int32), filled)


def pack_rows(values, target, padded):
    flat_rows = values.reshape(target.shape[0], values.shape[-1])
    return jnp.zeros((padded, flat_rows.shape[1]), flat_rows.dtype).at[target].set(flat_rows)


def plain_sum(products):
    running = 0.0
    for left_mat, right_mat in products:
        running = running + lax.dot_general(
            left_mat, right_mat, (((1,), (1,)), ((), ())), preferred_element_type=jnp.float32
        )
    return running


def expert_blocks(packed, packed_grads, filled, matrices, project):
    gate_mat, up_mat, down_mat = matrices
    padded, features = packed.shape
    width = gate_mat.shape[1]
    block_count = (filled + BLOCK - 1) // BLOCK
    contracted = (((0,), (0,)), ((), ()))

    def one_block(block, state_now):
        outputs, input_grads, hidden_all, gate_all, up_all = state_now
        offset = block * BLOCK
        rows_in = lax.dynamic_slice_in_dim(packed, offset, BLOCK, 0)
        cot_rows = lax.dynamic_slice_in_dim(packed_grads, offset, BLOCK, 0)
        pre_gate = jnp.dot(rows_in, gate_mat, preferred_element_type=jnp.float32)
        pre_up = jnp.dot(rows_in, up_mat, preferred_element_type=jnp.float32)
        hidden = (jax.nn.silu(pre_gate) * pre_up).astype(jnp.bfloat16)
        partial_value = project(((hidden, down_mat),)).astype(jnp.bfloat16)
        hidden_grad = jnp.dot(cot_rows, down_mat, preferred_element_type=jnp.float32)
        squash = jax.nn.sigmoid(pre_gate)
        gate_grad = (hidden_grad * pre_up * (squash * (1.0 + pre_gate * (1.0 - squash)))).astype(
            jnp.bfloat16
        )
        up_grad = (hidden_grad * (pre_gate * squash)).astype(jnp.bfloat16)
        input_part = project(((gate_grad, gate_mat), (up_grad, up_mat))).astype(jnp.bfloat16)
        outputs = lax.dynamic_update_slice_in_dim(outputs, partial_value, offset, 0)
        input_grads = lax.dynamic_update_slice_in_dim(input_grads, input_part, offset, 0)
        hidden_all = lax.dynamic_update_slice_in_dim(hidden_all, hidden, offset, 0)
        gate_all = lax.dynamic_update_slice_in_dim(gate_all, gate_grad, offset, 0)
        up_all = lax.dynamic_update_slice_in_dim(up_all, up_grad, offset, 0)
        return (outputs, input_grads, hidden_all, gate_all, up_all)

    zero_rows = jnp.zeros((padded, features), jnp.bfloat16)
    zero_hidden = jnp.zeros((padded, width), jnp.bfloat16)
    result = lax.fori_loop(
        0, block_count, one_block, (zero_rows, zero_rows, zero_hidden, zero_hidden, zero_hidden)
    )
    outputs, input_grads, hidden_all, gate_all, up_all = result
    gate_total = lax.dot_general(packed, gate_all, contracted, preferred_element_type=jnp.float32)
    up_total = lax.dot_general(packed, up_all, contracted, preferred_element_type=jnp.float32)
    down_total = lax.dot_general(
        packed_grads, hidden_all, contracted, preferred_element_type=jnp.float32
    )
    return (outputs, input_grads, (gate_total, up_total, down_total))


def shards(tokens, cotangent, expert_ids, gate_prob, gate_weight, up_weight, down_weight):
    experts = gate_weight.shape[0]
    tok_rows, features = tokens.shape
    pair_count = tok_rows * TOPK
    capacity = max(2, 5 * pair_count // (4 * experts))
    slot_of = slot_index(expert_ids, experts, capacity)
    gate_scale = gate_prob.reshape(-1)
    send_rows = (
        jnp.zeros((experts * capacity, features), jnp.bfloat16)
        .at[slot_of]
        .set(jnp.repeat(tokens, TOPK, axis=0))
    )
    scaled = (gate_scale[:, None] * jnp.repeat(cotangent, TOPK, axis=0).astype(jnp.float32)).astype(
        jnp.bfloat16
    )
    send_grads = jnp.zeros((experts * capacity, features), jnp.bfloat16).at[slot_of].set(scaled)
    send_flags = jnp.zeros((experts * capacity,), jnp.int32).at[slot_of].set(1)
    slot_shape = (experts, capacity, features)
    arrived, arrived_grads, arrived_flags = (
        lax.all_to_all(
            send_rows.reshape(slot_shape), "expert", split_axis=0, concat_axis=0, tiled=True
        ),
        lax.all_to_all(
            send_grads.reshape(slot_shape), "expert", split_axis=0, concat_axis=0, tiled=True
        ),
        lax.all_to_all(
            send_flags.reshape(experts, capacity), "expert", split_axis=0, concat_axis=0, tiled=True
        ),
    )
    resident = (
        lax.all_to_all(gate_weight, "expert", split_axis=0, concat_axis=1, tiled=True),
        lax.all_to_all(up_weight, "expert", split_axis=0, concat_axis=1, tiled=True),
        lax.all_to_all(down_weight, "expert", split_axis=0, concat_axis=1, tiled=True),
    )
    resident = (resident[0][0], resident[1][0], resident[2][0])
    gathered, gathered_grads, gathered_flags = (
        lax.all_gather(arrived, "dp", axis=0, tiled=True),
        lax.all_gather(arrived_grads, "dp", axis=0, tiled=True),
        lax.all_gather(arrived_flags, "dp", axis=0, tiled=True),
    )
    target, filled = packing(gathered_flags)
    padded = -(-target.shape[0] // BLOCK) * BLOCK
    outputs, input_grads, weight_grads = expert_blocks(
        pack_rows(gathered, target, padded),
        pack_rows(gathered_grads, target, padded),
        filled,
        resident,
        plain_sum,
    )
    back_shape = gathered.shape

    def return_rows(values):
        values = values[target].reshape(back_shape)
        summed = lax.psum_scatter(
            values.astype(jnp.float32).astype(jnp.bfloat16), "dp", scatter_dimension=0, tiled=True
        )
        return lax.all_to_all(summed, "expert", split_axis=0, concat_axis=0, tiled=True)

    out_home = return_rows(outputs)
    in_home = return_rows(input_grads)
    final_grads = tuple((total.astype(jnp.bfloat16)[None] for total in weight_grads))
    grad_gate, grad_up, grad_down = jax.tree.map(
        lambda part, own: part.astype(own.dtype),
        lax.all_to_all(shortened(final_grads), "expert", split_axis=1, concat_axis=0, tiled=True),
        final_grads,
    )
    out_pairs = out_home.reshape(experts * capacity, features)[slot_of].astype(jnp.float32)
    mixed_out = jnp.sum(
        (gate_scale[:, None] * out_pairs).reshape(tok_rows, TOPK, features), axis=1
    ).astype(jnp.bfloat16)
    in_pairs = in_home.reshape(experts * capacity, features)[slot_of].astype(jnp.float32)
    grad_tokens = jnp.sum(in_pairs.reshape(tok_rows, TOPK, features), axis=1).astype(jnp.bfloat16)
    return (mixed_out, grad_tokens, grad_gate, grad_up, grad_down)


def solution(mesh):
    placed = (
        P(("dp", "expert"), None),
        P(("dp", "expert"), None),
        P(("dp", "expert"), None),
        P(("dp", "expert"), None),
        P(None, "expert", "dp"),
        P(None, "expert", "dp"),
        P(None, "expert", "dp"),
    )
    return jax.shard_map(
        shards,
        mesh=mesh,
        in_specs=placed,
        out_specs=(
            P(("dp", "expert"), None),
            P(("dp", "expert"), None),
            P(None, "expert", "dp"),
            P(None, "expert", "dp"),
            P(None, "expert", "dp"),
        ),
        check_vma=False,
    )
```

profile of v0, /device:TPU:9, one launch (start us, length us, event | category | flops | bytes accessed | tf_op | source)
XLA Modules:
  0.0 698.3 jit_solution(8375048939023376230)
XLA Ops:
  19.3 34.8 %all_to_all.95 = bf16[8,40,2048]{2,1,0:T(8,128)(2,1)} all-to-all(bf16[8,40,2048]{2,1,0:T(8,128)(2,1)S(1)} %bitcast.102), channel_id=1, replica_groups=mesh['dp'=4,'expert'=8] {'expert'}, dimensions={0} | all-to-all | bytes 2621440 | tf_op jit(solution)/shard_map/all_to_all | solution.py:115
  57.8 35.3 %all_to_all.96 = bf16[8,40,2048]{2,1,0:T(8,128)(2,1)} all-to-all(bf16[8,40,2048]{2,1,0:T(8,128)(2,1)S(1)} %bitcast.103), channel_id=1, replica_groups=mesh['dp'=4,'expert'=8] {'expert'}, dimensions={0} | all-to-all | bytes 2621440 | tf_op jit(solution)/shard_map/all_to_all | solution.py:112
  94.6 9.3 %all_to_all.97 = s32[8,1,40]{2,1,0:T(1,128)S(1)} all-to-all(s32[8,1,40]{2,1,0:T(1,128)S(1)} %all_to_all.33), channel_id=1, replica_groups=mesh['dp'=4,'expert'=8] {'expert'}, dimensions={0} | all-to-all | bytes 2560 | tf_op jit(solution)/shard_map/all_to_all | solution.py:118
  104.0 38.2 %all_to_all.98 = bf16[8,256,352]{1,2,0:T(8,128)(2,1)S(1)} all-to-all(bf16[8,256,352]{1,2,0:T(8,128)(2,1)} %param.13), channel_id=1, replica_groups=mesh['dp'=4,'expert'=8] {'expert'}, dimensions={0} | all-to-all | bytes 2883584 | tf_op jit(solution)/shard_map/all_to_all | solution.py:123
  142.2 38.0 %all_to_all.99 = bf16[8,256,352]{1,2,0:T(8,128)(2,1)} all-to-all(bf16[8,256,352]{1,2,0:T(8,128)(2,1)S(1)} %copy-done.2), channel_id=1, replica_groups=mesh['dp'=4,'expert'=8] {'expert'}, dimensions={0} | all-to-all | bytes 2883584 | tf_op jit(solution)/shard_map/all_to_all | solution.py:124
  186.5 7.0 all-gather
  200.7 17.3 %all-to-all-done.4 = bf16[8,256,352]{1,2,0:T(8,128)(2,1)} async-done(((bf16[8,256,352]{1,2,0:T(8,128)(2,1)}), bf16[8,256,352]{1,2,0:T(8,128)(2,1)}, u32[]{:S(2)}, u32[]{:S(2)}) %all-to-all-start.4) | async-done | bytes 1441824 | tf_op jit(solution)/shard_map/all_to_all | solution.py:125
  220.5 14.0 %scatter_custom_fusion.4 = bf16[1280,2048]{1,0:T(8,128)(2,1)} fusion(s32[1280]{0:T(1024)S(1)} %fusion.28, bf16[1280,2048]{1,0:T(8,128)(2,1)} %bitcast.110, bf16[]{:T(256)} %constant.28.clone.1), kind=kCustom, calls=%fused_computation.34 | custom fusion | bytes 5243392 | tf_op jit(solution)/shard_map/scatter | solution.py:37
  234.6 14.2 %scatter_custom_fusion.2 = bf16[1280,2048]{1,0:T(8,128)(2,1)} fusion(s32[1280]{0:T(1024)S(1)} %fusion.28, bf16[1280,2048]{1,0:T(8,128)(2,1)} %bitcast.111, bf16[]{:T(256)} %constant.28.clone.1), kind=kCustom, calls=%fused_computation.36 | custom fusion | bytes 5243392 | tf_op jit(solution)/shard_map/scatter | solution.py:37
  257.6 97.6 %while.18 = (s32[]{:T(128)}, bf16[1280,2048]{1,0:T(8,128)(2,1)}, bf16[1280,2048]{1,0:T(8,128)(2,1)}, bf16[1280,352]{0,1:T(8,128)(2,1)}, bf16[1280,352]{0,1:T(8,1...) while((s32[]{:T(128)}, bf16[1280,2048]{1,0:T(8,128)(2,1)}, ...), condition=%wide.region_14.15_spmd, body=%wide.region_13.14_spmd.sunk | while | flops 1108758528 | bytes 20669680 | solution.py:81
  355.2 14.0 %gather_fusion.2 = bf16[1280,2048]{1,0:T(8,128)(2,1)} fusion(bf16[1280,2048]{1,0:T(8,128)(2,1)} %get-tuple-element.73, s32[2048]{0:T(1024)S(1)} %pad_clamp_fusion), kind=kCustom, calls=%fused_computation.2 | custom fusion | bytes 10490880 | tf_op jit(solution)/shard_map/gather | solution.py:145
  369.6 14.0 %gather_fusion = bf16[1280,2048]{1,0:T(8,128)(2,1)} fusion(bf16[1280,2048]{1,0:T(8,128)(2,1)} %get-tuple-element.72, s32[2048]{0:T(1024)S(1)} %pad_clamp_fusion), kind=kCustom, calls=%fused_computation | custom fusion | bytes 10490880 | tf_op jit(solution)/shard_map/gather | solution.py:145
  390.5 7.9 %copy.73 = bf16[1,2048,352]{2,0,1:T(2,128)(2,1)S(1)} copy(bf16[1,2048,352]{1,2,0:T(8,128)(2,1)} %fusion.19) | data formatting | bytes 2883584 | tf_op jit(solution)/shard_map/broadcast_in_dim | solution.py:153
  398.9 34.5 %reduce.20 = bf16[2048,352]{1,0:T(8,128)(2,1)} reduce(bf16[2048,1,352]{2,1,0:T(2,128)(2,1)S(1)} %bitcast.93, bf16[]{:T(256)} %broadcast.167), dimensions={1}, to_apply=%bitcast.51.reduce_sub_computation | reduce | bytes 2883586
  450.8 8.0 %copy.69 = bf16[1,2048,352]{2,0,1:T(2,128)(2,1)S(1)} copy(bf16[1,2048,352]{1,2,0:T(8,128)(2,1)} %fusion.17) | data formatting | bytes 2883584 | tf_op jit(solution)/shard_map/broadcast_in_dim | solution.py:153
  458.7 34.5 %reduce.18 = bf16[2048,352]{1,0:T(8,128)(2,1)} reduce(bf16[2048,1,352]{2,1,0:T(2,128)(2,1)S(1)} %bitcast.95, bf16[]{:T(256)} %broadcast.167), dimensions={1}, to_apply=%bitcast.47.reduce_sub_computation | reduce | bytes 2883586
  509.4 7.9 %copy.71 = bf16[1,2048,352]{2,0,1:T(2,128)(2,1)S(1)} copy(bf16[1,2048,352]{1,2,0:T(8,128)(2,1)} %fusion.18) | data formatting | bytes 2883584 | tf_op jit(solution)/shard_map/broadcast_in_dim | solution.py:153
  517.3 34.5 %reduce.19 = bf16[2048,352]{1,0:T(8,128)(2,1)} reduce(bf16[2048,1,352]{2,1,0:T(2,128)(2,1)S(1)} %bitcast.94, bf16[]{:T(256)} %broadcast.167), dimensions={1}, to_apply=%bitcast.49.reduce_sub_computation | reduce | bytes 2883586
  555.9 37.7 %all_to_all.100 = bf16[8,2,45056]{2,1,0:T(2,128)(2,1)} all-to-all(bf16[8,2,45056]{2,1,0:T(2,128)(2,1)S(1)} %reshape.357), channel_id=1, replica_groups=mesh['dp'=4,'expert'=8] {'expert'}, dimensions={0} | all-to-all | bytes 2883584 | tf_op jit(solution)/shard_map/all_to_all | solution.py:156
  599.5 28.6 %all-to-all-done.7 = bf16[8,40,2048]{2,1,0:T(8,128)(2,1)S(1)} async-done(((bf16[8,40,2048]{2,1,0:T(8,128)(2,1)}), bf16[8,40,2048]{2,1,0:T(8,128)(2,1)S(1)}, u32[]{:S(2)}, u32[]{:S(2)}) %all-to-all-start.7) | async-done | bytes 1310752 | tf_op jit(solution)/shard_map/all_to_all | solution.py:149
  628.1 7.3 %all-to-all-start.6 = ((bf16[8,40,2048]{2,1,0:T(8,128)(2,1)}), bf16[8,40,2048]{2,1,0:T(8,128)(2,1)S(1)}, u32[]{:S(2)}, u32[]{:S(2)}) async-start(bf16[8,40,2048]{2,1,0:T(8,128)(2,1)} %reduce-scatter.3.cloned.1.call-done), calls=%async_computation.7 | async-start | bytes 2621440 | tf_op jit(solution)/shard_map/all_to_all | solution.py:149
  635.5 7.0 %reshape.360 = bf16[2048,1,352]{2,1,0:T(2,128)(2,1)} reshape(bf16[8,2,45056]{2,1,0:T(2,128)(2,1)} %all-to-all-done.10) | data formatting | bytes 2883584
  648.3 7.0 %reshape.356 = bf16[2048,1,352]{2,1,0:T(2,128)(2,1)} reshape(bf16[8,2,45056]{2,1,0:T(2,128)(2,1)} %all-to-all-done.8) | data formatting | bytes 2883584
  661.2 7.0 %reshape.358 = bf16[2048,1,352]{2,1,0:T(2,128)(2,1)} reshape(bf16[8,2,45056]{2,1,0:T(2,128)(2,1)} %all_to_all.100) | data formatting | bytes 2883584
  (179 shorter events, 224.7 us)
Async XLA Ops:
  7.2 213.4 %all-gather.6.cloned.1.call-start = ((), (), s32[]{:S(2)}) async-start(), calls=%async_computation.14 | async-start | bytes 6553600 | tf_op jit(solution)/shard_map/all_gather | solution.py:130
  19.3 34.8 %copy-start.6 = (bf16[128,2048]{1,0:T(8,128)(2,1)S(1)}, bf16[128,2048]{1,0:T(8,128)(2,1)}, u32[]{:S(2)}) copy-start(bf16[128,2048]{1,0:T(8,128)(2,1)} %param.9) | copy-start | bytes 1572868
  54.1 180.4 %all-gather.4.cloned.1.call-start = ((), (), s32[]{:S(2)}) async-start(), calls=%async_computation.13 | async-start | bytes 6553600 | tf_op jit(solution)/shard_map/all_gather | solution.py:129
  93.1 49.1 %copy-start.2 = (bf16[8,256,352]{1,2,0:T(8,128)(2,1)S(1)}, bf16[8,256,352]{1,2,0:T(8,128)(2,1)}, u32[]{:S(2)}) copy-start(bf16[8,256,352]{1,2,0:T(8,128)(2,1)} %param.14) | copy-start | bytes 4325380
  180.2 37.7 %all-to-all-start.4 = ((bf16[8,256,352]{1,2,0:T(8,128)(2,1)}), bf16[8,256,352]{1,2,0:T(8,128)(2,1)}, u32[]{:S(2)}, u32[]{:S(2)}) async-start(bf16[8,256,352]{1,2,0:T(8,128)(2,1)} %param.15), calls=%async_computation.4 | async-start | bytes 2883584 | tf_op jit(solution)/shard_map/all_to_all | solution.py:125
  186.5 407.2 %reduce-scatter.5.cloned.1.call-start = ((), (), s32[]{:S(2)}) async-start(), calls=%async_computation.16 | async-start | bytes 6553600 | tf_op jit(solution)/shard_map/reduce_scatter | solution.py:146
  257.6 3.7 copy-start
  267.3 3.7 copy-start
  277.0 3.7 copy-start
  286.8 3.7 copy-start
  296.6 3.7 copy-start
  306.3 3.7 copy-start
  316.1 3.7 copy-start
  325.8 3.7 copy-start
  335.6 3.7 copy-start
  345.4 3.7 copy-start
  369.2 230.3 %reduce-scatter.3.cloned.1.call-start = ((), (), s32[]{:S(2)}) async-start(), calls=%async_computation.15 | async-start | bytes 6553600 | tf_op jit(solution)/shard_map/reduce_scatter | solution.py:146
  438.4 6.7 copy-start.4
  438.4 59.8 %all-to-all-start.10 = ((bf16[8,2,45056]{2,1,0:T(2,128)(2,1)}), bf16[8,2,45056]{2,1,0:T(2,128)(2,1)}, u32[]{:S(2)}, u32[]{:S(2)}) async-start(bf16[8,2,45056]{2,1,0:T(2,128)(2,1)} %reshape.359), calls=%async_computation.12 | async-start | bytes 2883584 | tf_op jit(solution)/shard_map/all_to_all | solution.py:156
  498.3 5.5 copy-start.5
  498.3 57.7 %all-to-all-start.8 = ((bf16[8,2,45056]{2,1,0:T(2,128)(2,1)}), bf16[8,2,45056]{2,1,0:T(2,128)(2,1)}, u32[]{:S(2)}, u32[]{:S(2)}) async-start(bf16[8,2,45056]{2,1,0:T(2,128)(2,1)} %reshape.355), calls=%async_computation.10 | async-start | bytes 2883584 | tf_op jit(solution)/shard_map/all_to_all | solution.py:156
  593.6 34.5 %all-to-all-start.7 = ((bf16[8,40,2048]{2,1,0:T(8,128)(2,1)}), bf16[8,40,2048]{2,1,0:T(8,128)(2,1)S(1)}, u32[]{:S(2)}, u32[]{:S(2)}) async-start(bf16[8,40,2048]{2,1,0:T(8,128)(2,1)} %reduce-scatter.5.cloned.1.call-done), calls=%async_computation.9 | async-start | bytes 2621440 | tf_op jit(solution)/shard_map/all_to_all | solution.py:149
  628.1 50.8 %all-to-all-start.6 = ((bf16[8,40,2048]{2,1,0:T(8,128)(2,1)}), bf16[8,40,2048]{2,1,0:T(8,128)(2,1)S(1)}, u32[]{:S(2)}, u32[]{:S(2)}) async-start(bf16[8,40,2048]{2,1,0:T(8,128)(2,1)} %reduce-scatter.3.cloned.1.call-done), calls=%async_computation.7 | async-start | bytes 2621440 | tf_op jit(solution)/shard_map/all_to_all | solution.py:149
  683.7 4.0 copy-start.1
  (1 other events, 1.2 us)
Sparse Core Ops, SparseCore 0:
  54.2 62.6 all-gather.5
  118.7 61.4 all-gather.3
  369.3 63.1 reduce-scatter.4
  435.3 61.4 reduce-scatter.2
where the time goes:
time: 709 us; the launch traced here: 698 us
  blocking collectives  200 us (28%)
  local copies, waits for them, and re-layouts  171 us (24%)
  other arithmetic  119 us (17%)
  matrix products  114 us (16%)
  waiting for transfers between devices  46 us (6%)
  starting transfers between devices  32.1 us (5%)
  between operations  15.1 us (2%)
    unnamed x4, other arithmetic  104 us
    unnamed x27, local copies, waits for them, and re-layouts  55.9 us
    all_to_all x1, blocking collectives, shards(): lax.all_to_all(gate_weight, 'expert', split_axis=0, concat_axis=1, tiled=...  38.2 us
    all_to_all x1, blocking collectives, shards(): lax.all_to_all(up_weight, 'expert', split_axis=0, concat_axis=1, tiled=True)  38 us
    all_to_all x1, blocking collectives, shards(): lax.all_to_all(shortened(final_grads), 'expert', split_axis=1, concat_axi...  37.7 us
    dot_general x30, matrix products, plain_sum(): lax.dot_general(left_mat, right_mat, (((1,), (1,)), ((), ())), preferred_...  35.8 us
    all_to_all x1, blocking collectives, shards(): lax.all_to_all(send_rows.reshape(slot_shape), 'expert', split_axis=0, con...  35.3 us
    all_to_all x1, blocking collectives, shards(): lax.all_to_all(send_grads.reshape(slot_shape), 'expert', split_axis=0, co...  34.8 us
  transfers between devices with their start and end apart: 9, of which 2 were waited for; matrix products, arithmetic and copies ran while one was open for 35% of the time, Pallas kernels for 0%

commit v1 on v0

v1 whole, which is shorter than its diff:
```python
import functools

import jax
import jax.numpy as jnp
from jax import lax
from jax.experimental import pallas as pl
from jax.experimental.pallas import tpu as pltpu
from jax.sharding import PartitionSpec as P

TOPK = 2
VMEM_BYTES = 56 * 1024 * 1024


def slot_index(expert_ids, experts, capacity):
    flat_ids = expert_ids.reshape(-1)
    one_hot = (flat_ids[:, None] == jnp.arange(experts, dtype=jnp.int32)[None, :]).astype(jnp.int32)
    before = jnp.cumsum(one_hot, axis=0) - one_hot
    return flat_ids * capacity + jnp.sum(before * one_hot, axis=1)


def greet(ne, nd):
    me, row = lax.axis_index("expert"), lax.axis_index("dp")
    barrier = pltpu.get_barrier_semaphore()

    @pl.loop(1, ne)
    def _(s):
        pl.semaphore_signal(barrier, inc=1, device_id={"expert": lax.rem(me + s, ne)})

    @pl.loop(1, nd)
    def _(r):
        pl.semaphore_signal(barrier, inc=1, device_id={"dp": lax.rem(row + r, nd)})

    pl.semaphore_wait(barrier, ne - 1 + nd - 1)


def dispatch_kernel(
    ne, nd,
    rows, grads, gate, up, down,
    rows_out, grads_out, gate_out, up_out, down_out,
    pair_send, pair_recv, weight_send, weight_recv, fan_send, fan_recv, local_sem,
):
    me, row = lax.axis_index("expert"), lax.axis_index("dp")
    pairs = ((rows, rows_out), (grads, grads_out))
    weights = ((gate, gate_out), (up, up_out), (down, down_out))

    def peer(s):
        return lax.rem(me + s, ne)

    def source(s):
        return lax.rem(me - s + ne, ne)

    def pair_copy(k, s, landing):
        return pltpu.make_async_remote_copy(
            src_ref=pairs[k][0].at[peer(s)], dst_ref=pairs[k][1].at[row, landing],
            send_sem=pair_send.at[k, s], recv_sem=pair_recv.at[k, s],
            device_id={"expert": peer(s)},
        )

    def weight_copy(k, s, landing):
        return pltpu.make_async_remote_copy(
            src_ref=weights[k][0].at[peer(s)], dst_ref=weights[k][1].at[landing],
            send_sem=weight_send.at[k, s], recv_sem=weight_recv.at[k, s],
            device_id={"expert": peer(s)},
        )

    def fan_copy(k, s, r, src, landing):
        return pltpu.make_async_remote_copy(
            src_ref=src, dst_ref=pairs[k][1].at[landing, source(s)],
            send_sem=fan_send.at[k, r, s], recv_sem=fan_recv.at[k, r, s],
            device_id={"dp": lax.rem(row + r, nd)},
        )

    greet(ne, nd)

    @pl.loop(1, ne)
    def _(s):
        for k in range(2):
            pair_copy(k, s, me).start()

    local = [
        pltpu.make_async_copy(pairs[k][0].at[me], pairs[k][1].at[row, me], local_sem.at[k])
        for k in range(2)
    ] + [
        pltpu.make_async_copy(weights[k][0].at[me], weights[k][1].at[me], local_sem.at[2 + k])
        for k in range(3)
    ]
    for copy in local:
        copy.start()
    for k in range(2):
        for r in range(1, nd):
            fan_copy(k, 0, r, pairs[k][0].at[me], row).start()

    @pl.loop(1, ne)
    def _(s):
        for k in range(2):
            pair_copy(k, s, source(s)).wait_recv()
            for r in range(1, nd):
                fan_copy(k, s, r, pairs[k][1].at[row, source(s)], row).start()
        for k in range(3):
            weight_copy(k, s, me).start()

    for copy in local:
        copy.wait()

    @pl.loop(0, ne)
    def _(s):
        for k in range(2):
            for r in range(1, nd):
                arrived = fan_copy(
                    k, s, r, pairs[k][1].at[row, source(s)], lax.rem(row - r + nd, nd)
                )
                arrived.wait_send()
                arrived.wait_recv()

    @pl.loop(1, ne)
    def _(s):
        for k in range(2):
            pair_copy(k, s, me).wait_send()
        for k in range(3):
            weight_copy(k, s, source(s)).wait()


def combine_kernel(
    ne, nd,
    outs, ins, gate, up, down,
    outs_home, ins_home, gate_out, up_out, down_out,
    own, arrived, summed,
    home_send, home_recv, weight_send, weight_recv, fan_send, fan_recv, own_sem, local_sem,
):
    me, row = lax.axis_index("expert"), lax.axis_index("dp")
    parts = ((outs, outs_home), (ins, ins_home))
    weights = ((gate, gate_out), (up, up_out), (down, down_out))

    def peer(s):
        return lax.rem(me + s, ne)

    def source(s):
        return lax.rem(me - s + ne, ne)

    def home_copy(k, s, landing):
        return pltpu.make_async_remote_copy(
            src_ref=summed.at[k, peer(s)], dst_ref=parts[k][1].at[landing],
            send_sem=home_send.at[k, s], recv_sem=home_recv.at[k, s],
            device_id={"expert": peer(s)},
        )

    def weight_copy(k, s, landing):
        return pltpu.make_async_remote_copy(
            src_ref=weights[k][0].at[peer(s)], dst_ref=weights[k][1].at[landing],
            send_sem=weight_send.at[k, s], recv_sem=weight_recv.at[k, s],
            device_id={"expert": peer(s)},
        )

    def fan_copy(k, s, r):
        to = lax.rem(row + r, nd)
        return pltpu.make_async_remote_copy(
            src_ref=parts[k][0].at[to, peer(s)], dst_ref=arrived.at[k, r - 1, peer(s)],
            send_sem=fan_send.at[k, r, s], recv_sem=fan_recv.at[k, r, s],
            device_id={"dp": to},
        )

    def own_copy(k, s):
        return pltpu.make_async_copy(
            parts[k][0].at[row, peer(s)], own.at[k, peer(s)], own_sem.at[k, s]
        )

    greet(ne, nd)

    @pl.loop(1, ne)
    def _(s):
        for k in range(3):
            weight_copy(k, s, me).start()

    @pl.loop(1, ne + 1)
    def _(step):
        s = lax.rem(step, ne)
        for k in range(2):
            for r in range(1, nd):
                fan_copy(k, s, r).start()
            own_copy(k, s).start()

    local = [
        pltpu.make_async_copy(weights[k][0].at[me], weights[k][1].at[me], local_sem.at[k])
        for k in range(3)
    ]
    for copy in local:
        copy.start()

    def add_up(s):
        for k in range(2):
            own_copy(k, s).wait()
            total = own[k, peer(s)].astype(jnp.float32)
            for r in range(1, nd):
                fan_copy(k, s, r).wait_recv()
                total = total + arrived[k, r - 1, peer(s)].astype(jnp.float32)
            summed[k, peer(s)] = total.astype(jnp.bfloat16)

    @pl.loop(1, ne)
    def _(s):
        add_up(s)
        for k in range(2):
            home_copy(k, s, me).start()

    add_up(0)
    mine = [
        pltpu.make_async_copy(summed.at[k, me], parts[k][1].at[me], local_sem.at[3 + k])
        for k in range(2)
    ]
    for copy in mine:
        copy.start()
    for copy in local + mine:
        copy.wait()

    @pl.loop(0, ne)
    def _(s):
        for k in range(2):
            for r in range(1, nd):
                fan_copy(k, s, r).wait_send()

    @pl.loop(1, ne)
    def _(s):
        for k in range(2):
            home_copy(k, s, source(s)).wait()
        for k in range(3):
            weight_copy(k, s, source(s)).wait()


def comm_call(kernel, ne, nd, args, out_shape, scratch, collective_id):
    anywhere = pl.BlockSpec(memory_space=pl.ANY)
    return pl.pallas_call(
        functools.partial(kernel, ne, nd),
        out_shape=out_shape,
        in_specs=[anywhere] * len(args),
        out_specs=[anywhere] * len(out_shape),
        scratch_shapes=scratch,
        compiler_params=pltpu.CompilerParams(
            collective_id=collective_id, has_side_effects=True, vmem_limit_bytes=VMEM_BYTES
        ),
    )(*args)


def shards(ne, nd, tokens, cotangent, expert_ids, gate_prob, gate_weight, up_weight, down_weight):
    experts, depth, width = gate_weight.shape
    tok_rows, features = tokens.shape
    pair_count = tok_rows * TOPK
    capacity = max(2, 5 * pair_count // (4 * experts))
    slot_of = slot_index(expert_ids, experts, capacity)
    gate_scale = gate_prob.reshape(-1)
    slots = experts * capacity
    send_rows = (
        jnp.zeros((slots, features), jnp.bfloat16).at[slot_of].set(jnp.repeat(tokens, TOPK, axis=0))
    )
    scaled = (gate_scale[:, None] * jnp.repeat(cotangent, TOPK, axis=0).astype(jnp.float32)).astype(
        jnp.bfloat16
    )
    send_grads = jnp.zeros((slots, features), jnp.bfloat16).at[slot_of].set(scaled)
    slot_shape = (experts, capacity, features)
    dma = pltpu.SemaphoreType.DMA
    pair_type = jax.ShapeDtypeStruct((nd,) + slot_shape, jnp.bfloat16)
    home_type = jax.ShapeDtypeStruct(slot_shape, jnp.bfloat16)
    weight_type = jax.ShapeDtypeStruct(gate_weight.shape, jnp.bfloat16)
    rows, grads, gate, up, down = comm_call(
        dispatch_kernel, ne, nd,
        (send_rows.reshape(slot_shape), send_grads.reshape(slot_shape),
         gate_weight, up_weight, down_weight),
        [pair_type] * 2 + [weight_type] * 3,
        [dma((2, ne)), dma((2, ne)), dma((3, ne)), dma((3, ne)),
         dma((2, nd, ne)), dma((2, nd, ne)), dma((5,))],
        0,
    )
    total = nd * slots
    rows, grads = rows.reshape(total, features), grads.reshape(total, features)
    gate, up, down = (part.reshape(features, width) for part in (gate, up, down))
    contracted = (((0,), (0,)), ((), ()))
    turned = (((1,), (1,)), ((), ()))

    def dot(left, right, dims=(((1,), (0,)), ((), ()))):
        return lax.dot_general(left, right, dims, preferred_element_type=jnp.float32)

    pre_gate = dot(rows, gate)
    pre_up = dot(rows, up)
    hidden_grad = dot(grads, down)
    squash = jax.nn.sigmoid(pre_gate)
    hidden = (pre_gate * squash * pre_up).astype(jnp.bfloat16)
    gate_grad = (hidden_grad * pre_up * (squash * (1.0 + pre_gate * (1.0 - squash)))).astype(
        jnp.bfloat16
    )
    up_grad = (hidden_grad * (pre_gate * squash)).astype(jnp.bfloat16)
    totals = tuple(
        dot(left, right, contracted).astype(jnp.bfloat16).reshape(gate_weight.shape)
        for left, right in ((rows, gate_grad), (rows, up_grad), (grads, hidden))
    )
    outputs = dot(hidden, down, turned).astype(jnp.bfloat16)
    input_grads = (dot(gate_grad, gate, turned) + dot(up_grad, up, turned)).astype(jnp.bfloat16)
    out_home, in_home, grad_gate, grad_up, grad_down = comm_call(
        combine_kernel, ne, nd,
        (outputs.reshape((nd,) + slot_shape), input_grads.reshape((nd,) + slot_shape)) + totals,
        [home_type] * 2 + [weight_type] * 3,
        [pltpu.VMEM((2,) + slot_shape, jnp.bfloat16),
         pltpu.VMEM((2, nd - 1) + slot_shape, jnp.bfloat16),
         pltpu.VMEM((2,) + slot_shape, jnp.bfloat16),
         dma((2, ne)), dma((2, ne)), dma((3, ne)), dma((3, ne)),
         dma((2, nd, ne)), dma((2, nd, ne)), dma((2, ne)), dma((5,))],
        1,
    )
    out_pairs = out_home.reshape(slots, features)[slot_of].astype(jnp.float32)
    mixed_out = jnp.sum(
        (gate_scale[:, None] * out_pairs).reshape(tok_rows, TOPK, features), axis=1
    ).astype(jnp.bfloat16)
    in_pairs = in_home.reshape(slots, features)[slot_of].astype(jnp.float32)
    grad_tokens = jnp.sum(in_pairs.reshape(tok_rows, TOPK, features), axis=1).astype(jnp.bfloat16)
    return (mixed_out, grad_tokens, grad_gate, grad_up, grad_down)


def solution(mesh):
    by_token = P(("dp", "expert"), None)
    by_block = P(None, "expert", "dp")
    return jax.shard_map(
        functools.partial(shards, mesh.shape["expert"], mesh.shape["dp"]),
        mesh=mesh,
        in_specs=(by_token,) * 4 + (by_block,) * 3,
        out_specs=(by_token,) * 2 + (by_block,) * 3,
        check_vma=False,
    )
```

time: 709 us -> 421 us (0.59)
  Pallas kernels: 0 us -> 327 us
  blocking collectives: 200 us -> 0 us
  local copies, waits for them, and re-layouts: 171 us -> 36.3 us
  other arithmetic: 119 us -> 13.4 us
  matrix products: 114 us -> 37.1 us
  waiting for transfers between devices: 46 us -> 0 us
  starting transfers between devices: 32.1 us -> 0 us
  between operations: 15.1 us -> 1.42 us
    pallas_call x0 -> x2, Pallas kernels: none -> 327 us  [comm_call(): pl.pallas_call(functools.partial(kernel, ne, nd), out_shape=out_shape, in...]
    all_to_all x6 -> x0, blocking collectives: 193 us -> none  [the longest x1 38.2 us: shards(): lax.all_to_all(gate_weight, 'expert', split_axis=0, concat_axis=1, tiled=...]
    unnamed x4 -> x1, other arithmetic: 104 us -> 0.01 us
    dot_general x63 -> x9, matrix products: 114 us -> 37.1 us  [dot(): lax.dot_general(left, right, dims, preferred_element_type=jnp.float32)]
    all_to_all x5 -> x0, waiting for transfers between devices: 45.9 us -> none  [the longest x2 28.7 us: return_rows(): lax.all_to_all(summed, 'expert', split_axis=0, concat_axis=0, tiled=True)]
    unnamed x27 -> x46, local copies, waits for them, and re-layouts: 55.9 us -> 13.8 us
    all_to_all x5 -> x0, starting transfers between devices: 31.6 us -> none  [the longest x2 13.1 us: return_rows(): lax.all_to_all(summed, 'expert', split_axis=0, concat_axis=0, tiled=True)]
    gather x5 -> x3, local copies, waits for them, and re-layouts: 35.3 us -> 5.92 us  [the longest x1 3.85 us: shards(): out_pairs = out_home.reshape(slots, features)[slot_of].astype(jnp.float32)]
  transfers between devices with their start and end apart: 9 -> 0, of which waited for: 2 -> 0; matrix products, arithmetic and copies ran while one was open for 35% -> 0% of each run, Pallas kernels for 0% -> 0%
where the time goes in v1:
time: 421 us; the launch traced here: 415 us
  Pallas kernels  327 us (78%)
  matrix products  37.1 us (9%)
  local copies, waits for them, and re-layouts  36.3 us (9%)
  other arithmetic  13.4 us (3%)
    pallas_call x2, Pallas kernels, comm_call(): pl.pallas_call(functools.partial(kernel, ne, nd), out_shape=out_shape, in...  327 us
    dot_general x9, matrix products, dot(): lax.dot_general(left, right, dims, preferred_element_type=jnp.float32)  37.1 us
    unnamed x46, local copies, waits for them, and re-layouts  13.8 us

profile of v1, /device:TPU:9, one launch (start us, length us, event | category | flops | bytes accessed | tf_op | source)
XLA Modules:
  0.0 415.0 jit_solution(9736611040348063101)
XLA Ops:
  5.2 2.1 broadcast_in_dim.5
  7.3 2.5 convert_element_type.57
  9.7 4.4 %scatter_custom_fusion.1 = bf16[320,2048]{1,0:T(8,128)(2,1)} fusion(s32[256]{0:T(256)S(1)} %bitcast.55, f32[256,2048]{1,0:T(8,128)} %convert_element_type.57, f32[256]{0:T(256)S(1)} %mul.65, bf16[]{:T(256)} %constant.6.clone.1), kind=kCustom, calls=%fused_computation.16 | custom fusion | flops 1048576 | bytes 3408898 | tf_op jit(solution)/shard_map/scatter | solution.py:256
  15.2 3.4 scatter_custom_fusion
  21.8 1.6 copy.29.down
  23.5 164.1 %shard_map.110 = (bf16[4,8,40,2048]{3,2,1,0:T(8,128)(2,1)}, bf16[4,8,40,2048]{3,2,1,0:T(8,128)(2,1)}, bf16[8,256,352]{2,1,0:T(8,128)(2,1)}, bf16[8,256,352]{2,1,0:T(8,128)(2,1)}, bf16[8,256,352]{2,1,0:T(8,128)(2,1)}) custom-call(bf16[8,40,2048]{2,1,0:T(8,128)(2,1)} %bitcast.49, bf16[8,40,2048]{2,1,0:T(8,128)(2,1)} %bitcast.48, ...), custom_call_target="tpu_custom_call" | custom-call | tf_op jit(solution)/shard_map/pallas_call | solution.py:230
  187.6 5.2 %fusion.10 = f32[1280,352]{0,1:T(8,128)S(1)} fusion(bf16[1280,2048]{1,0:T(8,128)(2,1)} %bitcast.59, bf16[2048,352]{1,0:T(8,128)(2,1)} %bitcast.53), kind=kOutput, calls=%fused_computation.32 | convolution fusion | flops 1845493760 | bytes 8486912 | tf_op jit(solution)/shard_map/dot_general | solution.py:278
  192.8 2.3 fusion.9
  195.1 4.2 %multiply_convert_fusion.1 = (bf16[1280,352]{0,1:T(8,128)(2,1)}, bf16[1280,352]{0,1:T(8,128)(2,1)}, bf16[1280,352]{0,1:T(8,128)(2,1)S(1)}) fusion(f32[1280,352]{0,1:T(8,128)S(1)} %fusion.9, f32[1280,352]{0,1:T(8,128)S(1)} %fusion.10, bf16[1280,2048]{1,0:T(8,128)(2,1)S(1)} %bitcast.65, bf16[2048,352]{1,0:T(8,128)(2,1)S(1)} %bitcast.67), kind=kOutput, calls=%fused_computation.11 | convolution fusion | flops 1852252160 | bytes 12992512 | tf_op jit(solution)/shard_map/dot_general | solution.py:278
  200.2 2.0 convolution_convert_fusion.1
  202.3 1.6 copy.32
  203.9 4.8 %convolution_convert_fusion.2 = bf16[2048,352]{0,1:T(8,128)(2,1)S(1)} fusion(bf16[1280,352]{0,1:T(8,128)(2,1)} %get-tuple-element.35, bf16[1280,2048]{1,0:T(8,128)(2,1)} %bitcast.60), kind=kOutput, calls=%fused_computation.7 | convolution fusion | flops 1846214656 | bytes 7585792 | tf_op jit(solution)/shard_map/dot_general | solution.py:278
  208.7 1.8 copy.31
  210.5 4.8 %convolution_convert_fusion.3 = bf16[2048,352]{0,1:T(8,128)(2,1)S(1)} fusion(bf16[1280,352]{0,1:T(8,128)(2,1)} %get-tuple-element.36, bf16[1280,2048]{1,0:T(8,128)(2,1)} %bitcast.61), kind=kOutput, calls=%fused_computation.8 | convolution fusion | flops 1846214656 | bytes 7585792 | tf_op jit(solution)/shard_map/dot_general | solution.py:278
  216.9 4.3 %fusion.11 = f32[1280,2048]{1,0:T(8,128)S(1)} fusion(bf16[1280,352]{0,1:T(8,128)(2,1)} %get-tuple-element.36, bf16[2048,352]{1,0:T(8,128)(2,1)S(1)} %bitcast.52), kind=kOutput, calls=%fused_computation.33 | convolution fusion | flops 1845493760 | bytes 12828672 | tf_op jit(solution)/shard_map/dot_general | solution.py:278
  221.2 4.8 %add_convert_fusion = bf16[1280,2048]{1,0:T(8,128)(2,1)} fusion(f32[1280,2048]{1,0:T(8,128)S(1)} %fusion.11, bf16[1280,352]{0,1:T(8,128)(2,1)S(1)} %copy-done.8, bf16[2048,352]{1,0:T(8,128)(2,1)S(1)} %bitcast.54), kind=kOutput, calls=%fused_computation.4 | convolution fusion | flops 1850736640 | bytes 18071552 | tf_op jit(solution)/shard_map/dot_general | solution.py:278
  226.0 4.7 %convolution_convert_fusion = bf16[1280,2048]{1,0:T(8,128)(2,1)} fusion(bf16[1280,352]{0,1:T(8,128)(2,1)S(1)} %copy-done.16, bf16[2048,352]{1,0:T(8,128)(2,1)S(1)} %bitcast.68), kind=kOutput, calls=%fused_computation.5 | convolution fusion | flops 1848115200 | bytes 7585792 | tf_op jit(solution)/shard_map/dot_general | solution.py:278
  230.7 162.8 %shard_map.111 = (bf16[8,40,2048]{2,1,0:T(8,128)(2,1)}, bf16[8,40,2048]{2,1,0:T(8,128)(2,1)}, bf16[8,256,352]{2,1,0:T(8,128)(2,1)}, bf16[8,256,352]{2,1,0:T(8,128)(2,1)}, bf16[8,256,352]{2,1,0:T(8,128)(2,1)}) custom-call(bf16[4,8,40,2048]{3,2,1,0:T(8,128)(2,1)} %bitcast.50, bf16[4,8,40,2048]{3,2,1,0:T(8,128)(2,1)} %bitcast.44, ...), custom_call_target="tpu_custom_call" | custom-call | tf_op jit(solution)/shard_map/pallas_call | solution.py:230
  393.5 3.8 gather_fusion
  397.4 1.6 reshape.131
  399.0 3.9 multiply_reduce_fusion
  405.0 3.6 reduce_sum.35
  408.7 2.7 copy.33
  412.9 1.6 copy.35
  (63 shorter events, 14.9 us)
Async XLA Ops:
  4.4 0.6 copy-start.9
  9.7 4.4 %copy-start.11 = (bf16[128,2048]{1,0:T(8,128)(2,1)S(1)}, bf16[128,2048]{1,0:T(8,128)(2,1)}, u32[]{:S(2)}) copy-start(bf16[128,2048]{1,0:T(8,128)(2,1)} %param.7) | copy-start | bytes 1572868
  14.8 3.9 copy-start.5
  18.7 1.6 copy-start.6
  20.3 1.5 copy-start.7
  187.5 5.2 %copy-start.1 = (bf16[8,256,352]{2,1,0:T(8,128)(2,1)S(1)}, bf16[8,256,352]{2,1,0:T(8,128)(2,1)}, u32[]{:S(2)}) copy-start(bf16[8,256,352]{2,1,0:T(8,128)(2,1)} %get-tuple-element.16) | copy-start | bytes 4325380
  187.5 5.2 %copy-start.12 = (bf16[4,8,40,2048]{3,2,1,0:T(8,128)(2,1)S(1)}, bf16[4,8,40,2048]{3,2,1,0:T(8,128)(2,1)}, u32[]{:S(2)}) copy-start(bf16[4,8,40,2048]{3,2,1,0:T(8,128)(2,1)} %get-tuple-element.15) | copy-start | bytes 15728644
  187.6 7.5 %slice-start = ((s8[5242880]{0:T(1024)(128)(4,1)}), s8[4194304]{0:T(1024)(128)(4,1)S(1)}, s32[]{:S(2)}) async-start(s8[5242880]{0:T(1024)(128)(4,1)} %bitcast.63), calls=%async_computation | async-start | bytes 8388608
  192.8 2.3 slice-start.1
  192.8 2.3 copy-start.13
  199.3 0.9 copy-start.15
  216.9 4.3 %copy-start.4 = (bf16[8,256,352]{2,1,0:T(8,128)(2,1)S(1)}, bf16[8,256,352]{2,1,0:T(8,128)(2,1)}, u32[]{:S(2)}) copy-start(bf16[8,256,352]{2,1,0:T(8,128)(2,1)} %get-tuple-element.17) | copy-start | bytes 4325380
  216.9 4.3 %copy-start.8 = (bf16[1280,352]{0,1:T(8,128)(2,1)S(1)}, bf16[1280,352]{0,1:T(8,128)(2,1)}, u32[]{:S(2)}) copy-start(bf16[1280,352]{0,1:T(8,128)(2,1)} %get-tuple-element.35) | copy-start | bytes 2703364
  221.2 4.8 %copy-start.14 = (bf16[8,256,352]{2,1,0:T(8,128)(2,1)S(1)}, bf16[8,256,352]{2,1,0:T(8,128)(2,1)}, u32[]{:S(2)}) copy-start(bf16[8,256,352]{2,1,0:T(8,128)(2,1)} %get-tuple-element.18) | copy-start | bytes 4325380
  221.2 4.8 %copy-start.16 = (bf16[1280,352]{0,1:T(8,128)(2,1)S(1)}, bf16[1280,352]{0,1:T(8,128)(2,1)}, u32[]{:S(2)}) copy-start(bf16[1280,352]{0,1:T(8,128)(2,1)} %copy-done.15) | copy-start | bytes 2703364
  397.4 1.6 copy-start.10
  399.0 4.0 copy-start
  408.7 2.7 copy-start.3
  411.3 1.6 copy-start.2

commit v2 on v1

--- a/solution.py
+++ b/solution.py
@@ -8,7 +8,7 @@
 from jax.sharding import PartitionSpec as P
 
 TOPK = 2
-VMEM_BYTES = 56 * 1024 * 1024
+VMEM_BYTES = 60 * 1024 * 1024
 
 
 def slot_index(expert_ids, experts, capacity):
@@ -31,6 +31,16 @@
         pl.semaphore_signal(barrier, inc=1, device_id={"dp": lax.rem(row + r, nd)})
 
     pl.semaphore_wait(barrier, ne - 1 + nd - 1)
+
+
+def weight_slot(ref, landing):
+    if len(ref.shape) == 3:
+        return ref.at[landing]
+    return ref.at[:, columns_of(landing, ref.shape[1] // lax.axis_size("expert"))]
+
+
+def columns_of(index, size):
+    return pl.ds(pl.multiple_of(index * size, size), size)
 
 
 def dispatch_kernel(
@@ -58,7 +68,7 @@
 
     def weight_copy(k, s, landing):
         return pltpu.make_async_remote_copy(
-            src_ref=weights[k][0].at[peer(s)], dst_ref=weights[k][1].at[landing],
+            src_ref=weights[k][0].at[peer(s)], dst_ref=weight_slot(weights[k][1], landing),
             send_sem=weight_send.at[k, s], recv_sem=weight_recv.at[k, s],
             device_id={"expert": peer(s)},
         )
@@ -81,7 +91,9 @@
         pltpu.make_async_copy(pairs[k][0].at[me], pairs[k][1].at[row, me], local_sem.at[k])
         for k in range(2)
     ] + [
-        pltpu.make_async_copy(weights[k][0].at[me], weights[k][1].at[me], local_sem.at[2 + k])
+        pltpu.make_async_copy(
+            weights[k][0].at[me], weight_slot(weights[k][1], me), local_sem.at[2 + k]
+        )
         for k in range(3)
     ]
     for copy in local:
@@ -223,6 +235,204 @@
             home_copy(k, s, source(s)).wait()
         for k in range(3):
             weight_copy(k, s, source(s)).wait()
+
+
+def fused_combine_kernel(
+    ne, nd,
+    rows, grads, gate, up, down, gate_grad, up_grad, hidden, gate_turned, up_turned, hidden_turned,
+    slots, scale,
+    mixed_out, token_out, gate_out, up_out, down_out,
+    rows_in, grads_in, gate_in, up_in, down_in, gate_grad_in, up_grad_in, hidden_in,
+    gate_turned_in, up_turned_in, hidden_turned_in,
+    made, part, arrived, summed, home,
+    home_send, home_recv, weight_send, weight_recv, fan_send, fan_recv, load_sem, local_sem,
+):
+    me, row = lax.axis_index("expert"), lax.axis_index("dp")
+    weight_outs = (gate_out, up_out, down_out)
+    features = rows.shape[1]
+    depth = features // ne
+    cap = part.shape[3]
+    block = ne * cap
+
+    def peer(s):
+        return lax.rem(me + s, ne)
+
+    def source(s):
+        return lax.rem(me - s + ne, ne)
+
+    def home_copy(k, s, landing):
+        return pltpu.make_async_remote_copy(
+            src_ref=summed.at[k, peer(s)], dst_ref=home.at[k, landing],
+            send_sem=home_send.at[k, s], recv_sem=home_recv.at[k, s],
+            device_id={"expert": peer(s)},
+        )
+
+    def weight_copy(k, s, landing):
+        return pltpu.make_async_remote_copy(
+            src_ref=made.at[k, peer(s)], dst_ref=weight_outs[k].at[landing],
+            send_sem=weight_send.at[k, s], recv_sem=weight_recv.at[k, s],
+            device_id={"expert": peer(s)},
+        )
+
+    def fan_copy(k, s, r):
+        to = lax.rem(row + r, nd)
+        return pltpu.make_async_remote_copy(
+            src_ref=part.at[k, to, peer(s)], dst_ref=arrived.at[k, r - 1, peer(s)],
+            send_sem=fan_send.at[k, r, s], recv_sem=fan_recv.at[k, r, s],
+            device_id={"dp": to},
+        )
+
+    loads = [
+        pltpu.make_async_copy(src, dst, load_sem.at[at])
+        for at, (src, dst) in enumerate((
+            (gate_turned, gate_turned_in), (rows, rows_in), (up_turned, up_turned_in),
+            (hidden_turned, hidden_turned_in), (grads, grads_in),
+            (hidden, hidden_in), (down, down_in), (gate_grad, gate_grad_in), (gate, gate_in),
+            (up_grad, up_grad_in), (up, up_in),
+        ))
+    ]
+    for load in loads:
+        load.start()
+    greet(ne, nd)
+    for load in loads:
+        load.wait()
+
+    def dot(left, right):
+        return jnp.dot(left, right, preferred_element_type=jnp.float32)
+
+    def make_weights(s):
+        columns = columns_of(peer(s), depth)
+        rows_now, grads_now = rows_in[:, columns], grads_in[:, columns]
+        made[0, peer(s)] = dot(gate_turned_in[...], rows_now).astype(jnp.bfloat16)
+        made[1, peer(s)] = dot(up_turned_in[...], rows_now).astype(jnp.bfloat16)
+        made[2, peer(s)] = dot(hidden_turned_in[...], grads_now).astype(jnp.bfloat16)
+
+    def make_parts(to):
+        lines = columns_of(to, block)
+
+        @pl.loop(0, features // 256)
+        def _(tile):
+            columns = columns_of(tile, 256)
+            outs = dot(hidden_in[lines, :], down_in[:, columns])
+            ins = dot(gate_grad_in[lines, :], gate_in[:, columns]) + dot(
+                up_grad_in[lines, :], up_in[:, columns]
+            )
+            for e in range(ne):
+                part[0, to, e, :, columns] = outs[e * cap : (e + 1) * cap].astype(jnp.bfloat16)
+                part[1, to, e, :, columns] = ins[e * cap : (e + 1) * cap].astype(jnp.bfloat16)
+
+    @pl.loop(1, ne)
+    def _(s):
+        make_weights(s)
+        for k in range(3):
+            weight_copy(k, s, me).start()
+
+        @pl.when(s < nd)
+        def _():
+            make_parts(lax.rem(row + s, nd))
+
+            @pl.loop(1, ne + 1)
+            def _(step):
+                for k in range(2):
+                    fan_copy(k, lax.rem(step, ne), s).start()
+
+    make_parts(row)
+    make_weights(0)
+    local = [
+        pltpu.make_async_copy(made.at[k, me], weight_outs[k].at[me], local_sem.at[k])
+        for k in range(3)
+    ]
+    for copy in local:
+        copy.start()
+
+    def add_up(s, target):
+        for k in range(2):
+            for r in range(1, nd):
+                fan_copy(k, s, r).wait_recv()
+
+            @pl.loop(0, features // 256)
+            def _(tile):
+                columns = columns_of(tile, 256)
+                total = part[k, row, peer(s), :, columns].astype(jnp.float32)
+                for r in range(1, nd):
+                    total = total + arrived[k, r - 1, peer(s), :, columns].astype(jnp.float32)
+                target[k, peer(s), :, columns] = total.astype(jnp.bfloat16)
+
+    @pl.loop(1, ne)
+    def _(s):
+        add_up(s, summed)
+        for k in range(2):
+            home_copy(k, s, me).start()
+
+    add_up(0, home)
+    for copy in local:
+        copy.wait()
+
+    @pl.loop(0, ne)
+    def _(s):
+        for k in range(2):
+            for r in range(1, nd):
+                fan_copy(k, s, r).wait_send()
+
+    @pl.loop(1, ne)
+    def _(s):
+        for k in range(2):
+            home_copy(k, s, source(s)).wait()
+
+    tok_rows = slots.shape[0]
+    places = lax.broadcasted_iota(jnp.int32, (tok_rows, block), 1)
+    chosen = [
+        jnp.where(places == slots[:, k : k + 1], 1.0, 0.0).astype(jnp.float32) for k in range(TOPK)
+    ]
+    either = (chosen[0] + chosen[1]).astype(jnp.bfloat16)
+    first, second = (one.astype(jnp.bfloat16) for one in chosen)
+    first_scale, second_scale = scale[:, 0:1], scale[:, 1:2]
+
+    def at_home(k, columns):
+        return jnp.concatenate(
+            [home[k, e, :, columns].astype(jnp.float32) for e in range(ne)], axis=0
+        ).astype(jnp.bfloat16)
+
+    @pl.loop(0, features // 256)
+    def _(tile):
+        columns = columns_of(tile, 256)
+        outs = at_home(0, columns)
+        mixed_out[:, columns] = (
+            first_scale * dot(first, outs) + second_scale * dot(second, outs)
+        ).astype(jnp.bfloat16)
+        token_out[:, columns] = dot(either, at_home(1, columns)).astype(jnp.bfloat16)
+
+    @pl.loop(1, ne)
+    def _(s):
+        for k in range(3):
+            weight_copy(k, s, source(s)).wait()
+
+
+def fused_combine(ne, nd, capacity, args, weight_type):
+    rows, gate, turned, slots = args[0], args[2], args[8], args[11]
+    features = rows.shape[1]
+    anywhere, inside = pl.BlockSpec(memory_space=pl.ANY), pl.BlockSpec(memory_space=pltpu.VMEM)
+    token_type = jax.ShapeDtypeStruct((slots.shape[0], features), jnp.bfloat16)
+    dma = pltpu.SemaphoreType.DMA
+    block = (ne, capacity, features)
+    return pl.pallas_call(
+        functools.partial(fused_combine_kernel, ne, nd),
+        out_shape=[token_type] * 2 + [weight_type] * 3,
+        in_specs=[anywhere] * 11 + [inside] * 2,
+        out_specs=[inside] * 2 + [anywhere] * 3,
+        scratch_shapes=[pltpu.VMEM(part.shape, part.dtype) for part in args[:11]] + [
+            pltpu.VMEM((3,) + weight_type.shape, jnp.bfloat16),
+            pltpu.VMEM((2, nd) + block, jnp.bfloat16),
+            pltpu.VMEM((2, nd - 1) + block, jnp.bfloat16),
+            pltpu.VMEM((2,) + block, jnp.bfloat16),
+            pltpu.VMEM((2,) + block, jnp.bfloat16),
+            dma((2, ne)), dma((2, ne)), dma((3, ne)), dma((3, ne)),
+            dma((2, nd, ne)), dma((2, nd, ne)), dma((11,)), dma((3,)),
+        ],
+        compiler_params=pltpu.CompilerParams(
+            collective_id=1, has_side_effects=True, vmem_limit_bytes=VMEM_BYTES
+        ),
+    )(*args)
 
 
 def comm_call(kernel, ne, nd, args, out_shape, scratch, collective_id):
@@ -258,34 +468,50 @@
     dma = pltpu.SemaphoreType.DMA
     pair_type = jax.ShapeDtypeStruct((nd,) + slot_shape, jnp.bfloat16)
     home_type = jax.ShapeDtypeStruct(slot_shape, jnp.bfloat16)
-    weight_type = jax.ShapeDtypeStruct(gate_weight.shape, jnp.bfloat16)
+    aligned = depth % 256 == 0 and capacity % 8 == 0 and width % 16 == 0
+    weights = (gate_weight, up_weight, down_weight)
+    if aligned:
+        weights = tuple(part.transpose(0, 2, 1) for part in weights)
+        landed_type = jax.ShapeDtypeStruct((width, features), jnp.bfloat16)
+    else:
+        landed_type = jax.ShapeDtypeStruct(gate_weight.shape, jnp.bfloat16)
+    weight_type = jax.ShapeDtypeStruct(weights[0].shape, jnp.bfloat16)
     rows, grads, gate, up, down = comm_call(
         dispatch_kernel, ne, nd,
-        (send_rows.reshape(slot_shape), send_grads.reshape(slot_shape),
-         gate_weight, up_weight, down_weight),
-        [pair_type] * 2 + [weight_type] * 3,
+        (send_rows.reshape(slot_shape), send_grads.reshape(slot_shape)) + weights,
+        [pair_type] * 2 + [landed_type] * 3,
         [dma((2, ne)), dma((2, ne)), dma((3, ne)), dma((3, ne)),
          dma((2, nd, ne)), dma((2, nd, ne)), dma((5,))],
         0,
     )
     total = nd * slots
     rows, grads = rows.reshape(total, features), grads.reshape(total, features)
-    gate, up, down = (part.reshape(features, width) for part in (gate, up, down))
+    if not aligned:
+        gate, up, down = (part.reshape(features, width) for part in (gate, up, down))
     contracted = (((0,), (0,)), ((), ()))
     turned = (((1,), (1,)), ((), ()))
 
-    def dot(left, right, dims=(((1,), (0,)), ((), ()))):
+    def dot(left, right, dims):
         return lax.dot_general(left, right, dims, preferred_element_type=jnp.float32)
 
-    pre_gate = dot(rows, gate)
-    pre_up = dot(rows, up)
-    hidden_grad = dot(grads, down)
+    ahead = turned if aligned else (((1,), (0,)), ((), ()))
+    pre_gate = dot(rows, gate, ahead)
+    pre_up = dot(rows, up, ahead)
+    hidden_grad = dot(grads, down, ahead)
     squash = jax.nn.sigmoid(pre_gate)
     hidden = (pre_gate * squash * pre_up).astype(jnp.bfloat16)
     gate_grad = (hidden_grad * pre_up * (squash * (1.0 + pre_gate * (1.0 - squash)))).astype(
         jnp.bfloat16
     )
     up_grad = (hidden_grad * (pre_gate * squash)).astype(jnp.bfloat16)
+    if aligned:
+        mixed_out, grad_tokens, *weight_grads = fused_combine(
+            ne, nd, capacity,
+            (rows, grads, gate, up, down, gate_grad, up_grad, hidden,
+             gate_grad.T, up_grad.T, hidden.T, slot_of.reshape(tok_rows, TOPK), gate_prob),
+            weight_type,
+        )
+        return (mixed_out, grad_tokens, *(part.transpose(0, 2, 1) for part in weight_grads))
     totals = tuple(
         dot(left, right, contracted).astype(jnp.bfloat16).reshape(gate_weight.shape)
         for left, right in ((rows, gate_grad), (rows, up_grad), (grads, hidden))

time: 421 us -> 375 us (0.89); the launches traced: 415 us -> 375 us
  matrix products: 37.1 us -> 10.5 us
  Pallas kernels: 327 us -> 320 us
  local copies, waits for them, and re-layouts: 36.3 us -> 29.9 us
    pallas_call x2 -> x1, Pallas kernels: 327 us -> 156 us  [comm_call(): pl.pallas_call(functools.partial(kernel, ne, nd), out_shape=out_shape, in...]
    pallas_call x0 -> x1, Pallas kernels: none -> 164 us  [fused_combine(): pl.pallas_call(functools.partial(fused_combine_kernel, ne, nd), out_shape...]
    dot_general x9 -> x3, matrix products: 37.1 us -> 10.5 us  [dot(): lax.dot_general(left, right, dims, preferred_element_type=jnp.float32)]
    dot_general x0 -> x3, local copies, waits for them, and re-layouts: none -> 8.49 us  [dot(): lax.dot_general(left, right, dims, preferred_element_type=jnp.float32)]
    convert_element_type x0 -> x2, other arithmetic: none -> 7.65 us  [shards(): hidden = (pre_gate * squash * pre_up).astype(jnp.bfloat16)]
    reduce_sum x2 -> x0, other arithmetic: 7.58 us -> none  [the longest x1 3.94 us: shards(): jnp.sum((gate_scale[:, None] * out_pairs).reshape(tok_rows, TOPK, feature...]
    convert_element_type x4 -> x0, local copies, waits for them, and re-layouts: 6.58 us -> none  [the longest x3 4.99 us: shards(): dot(left, right, contracted).astype(jnp.bfloat16).reshape(gate_weight.shape)]
    gather x3 -> x0, local copies, waits for them, and re-layouts: 5.92 us -> none  [the longest x1 3.85 us: shards(): out_pairs = out_home.reshape(slots, features)[slot_of].astype(jnp.float32)]
where the time goes in v2:
time: 375 us
  Pallas kernels  320 us (85%)
  local copies, waits for them, and re-layouts  29.9 us (8%)
  other arithmetic  13.4 us (4%)
  matrix products  10.5 us (3%)
    pallas_call x1, Pallas kernels, fused_combine(): pl.pallas_call(functools.partial(fused_combine_kernel, ne, nd), out_shape...  164 us
    pallas_call x1, Pallas kernels, comm_call(): pl.pallas_call(functools.partial(kernel, ne, nd), out_shape=out_shape, in...  156 us
    dot_general x3, matrix products, dot(): lax.dot_general(left, right, dims, preferred_element_type=jnp.float32)  10.5 us
    unnamed x33, local copies, waits for them, and re-layouts  9.69 us
    dot_general x3, local copies, waits for them, and re-layouts, dot(): lax.dot_general(left, right, dims, preferred_element_type=jnp.float32)  8.49 us
    convert_element_type x2, other arithmetic, shards(): hidden = (pre_gate * squash * pre_up).astype(jnp.bfloat16)  7.65 us

profile of v2, /device:TPU:9, one launch (start us, length us, event | category | flops | bytes accessed | tf_op | source)
XLA Modules:
  0.0 374.7 jit_solution(6857766073756045417)
XLA Ops:
  0.6 0.8 copy.33
  2.8 0.6 fusion.18
  3.6 0.8 copy.36.scale
  4.5 2.1 broadcast_in_dim.10
  6.6 2.5 convert_element_type.35
  9.1 4.4 %scatter_custom_fusion.1 = bf16[320,2048]{1,0:T(8,128)(2,1)} fusion(s32[256]{0:T(256)S(1)} %bitcast.80, f32[256,2048]{1,0:T(8,128)} %convert_element_type.35, f32[256]{0:T(256)S(1)} %mul.78, bf16[]{:T(256)} %constant.5.clone.1), kind=kCustom, calls=%fused_computation.23 | custom fusion | flops 1048576 | bytes 3408898 | tf_op jit(solution)/shard_map/scatter | solution.py:466
  14.6 3.3 scatter_custom_fusion
  17.9 155.6 %shard_map.110 = (bf16[4,8,40,2048]{3,2,1,0:T(8,128)(2,1)}, bf16[4,8,40,2048]{3,2,1,0:T(8,128)(2,1)}, bf16[352,2048]{1,0:T(8,128)(2,1)}, bf16[352,2048]{1,0:T(8,128)(2,1)}, bf16[352,2048]{1,0:T(8,128)(2,1)}) custom-call(bf16[8,40,2048]{2,1,0:T(8,128)(2,1)} %bitcast.65, bf16[8,40,2048]{2,1,0:T(8,128)(2,1)} %bitcast.64, bf16[8,352,256]{2,1,0:T(8,128)(2,1)} %bitcast.76, ...), custom_call_target="tpu_custom_call" | custom-call | tf_op jit(solution)/shard_map/pallas_call | solution.py:440
  173.6 5.1 %fusion.20 = f32[1280,352]{0,1:T(8,128)S(1)} fusion(bf16[1280,2048]{1,0:T(8,128)(2,1)} %bitcast.66, bf16[352,2048]{1,0:T(8,128)(2,1)} %get-tuple-element.18.up), kind=kOutput, calls=%fused_computation.39 | convolution fusion | flops 1845493760 | bytes 8486912 | tf_op jit(solution)/shard_map/dot_general | solution.py:495
  178.7 3.3 fusion.19
  182.0 2.1 fusion.21
  184.1 2.5 fusion.8
  186.7 1.9 copy.39
  188.5 2.8 copy.41
  191.4 2.8 copy.37
  194.2 2.8 copy.42
  197.0 5.1 %multiply_convert_fusion.1 = (bf16[1280,352]{1,0:T(8,128)(2,1)}, bf16[1280,352]{1,0:T(8,128)(2,1)}, bf16[1280,352]{1,0:T(8,128)(2,1)}) fusion(f32[1280,352]{1,0:T(8,128)} %copy.42, f32[1280,352]{1,0:T(8,128)} %copy.37, f32[1280,352]{1,0:T(8,128)S(1)} %copy.39, f32[1280,352]{1,0:T(8,128)} %copy.41), kind=kLoop, calls=%fused_computation.3 | loop fusion | flops 6307840 | bytes 9912320 | tf_op jit(solution)/shard_map/convert_element_type | solution.py:502
  202.2 164.4 %shard_map.111 = (bf16[128,2048]{1,0:T(8,128)(2,1)}, bf16[128,2048]{1,0:T(8,128)(2,1)}, bf16[8,352,256]{2,1,0:T(8,128)(2,1)}, bf16[8,352,256]{2,1,0:T(8,128)(2,1)}, bf16[8,352,256]{2,1,0:T(8,128)(2,1)}) custom-call(bf16[1280,2048]{1,0:T(8,128)(2,1)} %bitcast.67, bf16[1280,2048]{1,0:T(8,128)(2,1)} %bitcast.71, bf16[352,2048]{1,0:T(8,128)(2,1)} %get-tuple-element.17.gate, ...), custom_call_target="tpu_custom_call" | custom-call | tf_op jit(solution)/shard_map/pallas_call | solution.py:418
  366.6 2.0 copy.49
  368.6 2.0 copy.50
  370.6 1.1 copy.51
  371.7 1.1 copy.52
  372.8 0.8 copy-done.4
  373.6 1.1 copy.53
  (40 shorter events, 2.8 us)
Async XLA Ops:
  4.4 4.7 %copy-start.9 = (f32[128,2]{1,0:T(8,128)}, f32[128,2]{1,0:T(8,128)S(1)}, u32[]{:S(2)}) copy-start(f32[128,2]{1,0:T(8,128)S(1)} %copy.36.scale) | copy-start | bytes 3076
  9.1 4.4 %copy-start.10 = (bf16[128,2048]{1,0:T(8,128)(2,1)S(1)}, bf16[128,2048]{1,0:T(8,128)(2,1)}, u32[]{:S(2)}) copy-start(bf16[128,2048]{1,0:T(8,128)(2,1)} %param.7) | copy-start | bytes 1572868
  173.5 5.2 %copy-start.3 = (bf16[4,8,40,2048]{3,2,1,0:T(8,128)(2,1)S(1)}, bf16[4,8,40,2048]{3,2,1,0:T(8,128)(2,1)}, u32[]{:S(2)}) copy-start(bf16[4,8,40,2048]{3,2,1,0:T(8,128)(2,1)} %get-tuple-element.16) | copy-start | bytes 15728644
  173.5 5.2 %copy-start.8 = (bf16[352,2048]{1,0:T(8,128)(2,1)S(1)}, bf16[352,2048]{1,0:T(8,128)(2,1)}, u32[]{:S(2)}) copy-start(bf16[352,2048]{1,0:T(8,128)(2,1)} %get-tuple-element.19.down) | copy-start | bytes 4325380
  173.5 8.5 %slice-start = ((s8[5242880]{0:T(1024)(128)(4,1)}), s8[4194304]{0:T(1024)(128)(4,1)S(1)}, s32[]{:S(2)}) async-start(s8[5242880]{0:T(1024)(128)(4,1)} %bitcast.68), calls=%async_computation | async-start | bytes 8388608
  178.7 5.4 %copy-start = (f32[1280,352]{0,1:T(8,128)}, f32[1280,352]{0,1:T(8,128)S(1)}, u32[]{:S(2)}) copy-start(f32[1280,352]{0,1:T(8,128)S(1)} %fusion.20) | copy-start | bytes 5406724
  178.7 3.3 slice-start.1
  178.7 3.3 copy-start.7
  182.0 2.1 copy-start.1
  184.1 2.5 copy-start.2
  366.6 4.0 %copy-start.6 = (bf16[8,352,256]{2,1,0:T(8,128)(2,1)S(1)}, bf16[8,352,256]{2,1,0:T(8,128)(2,1)}, u32[]{:S(2)}) copy-start(bf16[8,352,256]{2,1,0:T(8,128)(2,1)} %get-tuple-element.22) | copy-start | bytes 4325380
  368.6 3.1 copy-start.5
  371.7 1.9 copy-start.4

commit v3 on v2

--- a/solution.py
+++ b/solution.py
@@ -37,6 +37,16 @@
     if len(ref.shape) == 3:
         return ref.at[landing]
     return ref.at[:, columns_of(landing, ref.shape[1] // lax.axis_size("expert"))]
+
+
+def dot(left, right):
+    return jnp.dot(left, right, preferred_element_type=jnp.float32)
+
+
+def dot_turned(left, right):
+    return lax.dot_general(
+        left, right, (((1,), (1,)), ((), ())), preferred_element_type=jnp.float32
+    )
 
 
 def columns_of(index, size):
@@ -130,6 +140,154 @@
             pair_copy(k, s, me).wait_send()
         for k in range(3):
             weight_copy(k, s, source(s)).wait()
+
+
+def fused_dispatch_kernel(
+    ne, nd,
+    tokens, cotangent, ids_turned, scale, gate, up, down,
+    rows_out, grads_out, gate_out, up_out, down_out,
+    rows, grads,
+    pair_send, pair_recv, weight_send, weight_recv, fan_send, fan_recv, local_sem,
+):
+    me, row = lax.axis_index("expert"), lax.axis_index("dp")
+    pairs = ((rows, rows_out), (grads, grads_out))
+    weights = ((gate, gate_out), (up, up_out), (down, down_out))
+
+    early = min(3, ne)
+
+    def peer(s):
+        return lax.rem(me + s, ne)
+
+    def source(s):
+        return lax.rem(me - s + ne, ne)
+
+    def pair_copy(k, s, landing):
+        return pltpu.make_async_remote_copy(
+            src_ref=pairs[k][0].at[peer(s)], dst_ref=pairs[k][1].at[row, landing],
+            send_sem=pair_send.at[k, s], recv_sem=pair_recv.at[k, s],
+            device_id={"expert": peer(s)},
+        )
+
+    def weight_copy(k, s, landing):
+        return pltpu.make_async_remote_copy(
+            src_ref=weights[k][0].at[peer(s)], dst_ref=weight_slot(weights[k][1], landing),
+            send_sem=weight_send.at[k, s], recv_sem=weight_recv.at[k, s],
+            device_id={"expert": peer(s)},
+        )
+
+    def fan_copy(k, s, r, src, landing):
+        return pltpu.make_async_remote_copy(
+            src_ref=src, dst_ref=pairs[k][1].at[landing, source(s)],
+            send_sem=fan_send.at[k, r, s], recv_sem=fan_recv.at[k, r, s],
+            device_id={"dp": lax.rem(row + r, nd)},
+        )
+
+    greet(ne, nd)
+
+    @pl.loop(1, early)
+    def _(s):
+        for k in range(3):
+            weight_copy(k, s, me).start()
+
+    cap, features = rows.shape[1:]
+    tok_rows = tokens.shape[0]
+    experts = lax.broadcasted_iota(jnp.int32, (ne, tok_rows), 0)
+    named = [jnp.where(experts == ids_turned[k : k + 1, :], 1.0, 0.0) for k in range(TOPK)]
+    earlier = jnp.where(
+        lax.broadcasted_iota(jnp.int32, (tok_rows, tok_rows), 0)
+        < lax.broadcasted_iota(jnp.int32, (tok_rows, tok_rows), 1), 1.0, 0.0
+    ).astype(jnp.bfloat16)
+    rank = dot((named[0] + named[1]).astype(jnp.bfloat16), earlier)
+    place = rank + (experts * cap).astype(jnp.float32)
+    slots = lax.broadcasted_iota(jnp.int32, (ne * cap, tok_rows), 0).astype(jnp.float32)
+    first, second = (
+        jnp.where(slots == jnp.sum(one * place, axis=0, keepdims=True), 1.0, 0.0) for one in named
+    )
+    either = (first + second).astype(jnp.bfloat16)
+    first, second = first.astype(jnp.bfloat16), second.astype(jnp.bfloat16)
+
+    @pl.loop(0, features // 256)
+    def _(tile):
+        columns = columns_of(tile, 256)
+        cot = cotangent[:, columns].astype(jnp.float32)
+        picked = dot(either, tokens[:, columns])
+        picked_grads = dot(first, (scale[:, 0:1] * cot).astype(jnp.bfloat16)) + dot(
+            second, (scale[:, 1:2] * cot).astype(jnp.bfloat16)
+        )
+        for e in range(ne):
+            rows[e, :, columns] = picked[e * cap : (e + 1) * cap].astype(jnp.bfloat16)
+            grads[e, :, columns] = picked_grads[e * cap : (e + 1) * cap].astype(jnp.bfloat16)
+
+    @pl.loop(1, ne)
+    def _(s):
+        for k in range(2):
+            pair_copy(k, s, me).start()
+
+    local = [
+        pltpu.make_async_copy(pairs[k][0].at[me], pairs[k][1].at[row, me], local_sem.at[k])
+        for k in range(2)
+    ] + [
+        pltpu.make_async_copy(
+            weights[k][0].at[me], weight_slot(weights[k][1], me), local_sem.at[2 + k]
+        )
+        for k in range(3)
+    ]
+    for copy in local:
+        copy.start()
+    for k in range(2):
+        for r in range(1, nd):
+            fan_copy(k, 0, r, pairs[k][0].at[me], row).start()
+
+    @pl.loop(1, ne)
+    def _(s):
+        for k in range(2):
+            pair_copy(k, s, source(s)).wait_recv()
+            for r in range(1, nd):
+                fan_copy(k, s, r, pairs[k][1].at[row, source(s)], row).start()
+        @pl.when(s >= early)
+        def _():
+            for k in range(3):
+                weight_copy(k, s, me).start()
+
+    for copy in local:
+        copy.wait()
+
+    @pl.loop(0, ne)
+    def _(s):
+        for k in range(2):
+            for r in range(1, nd):
+                arrived = fan_copy(
+                    k, s, r, pairs[k][1].at[row, source(s)], lax.rem(row - r + nd, nd)
+                )
+                arrived.wait_send()
+                arrived.wait_recv()
+
+    @pl.loop(1, ne)
+    def _(s):
+        for k in range(2):
+            pair_copy(k, s, me).wait_send()
+        for k in range(3):
+            weight_copy(k, s, source(s)).wait()
+
+
+def fused_dispatch(ne, nd, capacity, args, pair_type, landed_type):
+    anywhere, inside = pl.BlockSpec(memory_space=pl.ANY), pl.BlockSpec(memory_space=pltpu.VMEM)
+    dma = pltpu.SemaphoreType.DMA
+    block = pair_type.shape[1:]
+    return pl.pallas_call(
+        functools.partial(fused_dispatch_kernel, ne, nd),
+        out_shape=[pair_type] * 2 + [landed_type] * 3,
+        in_specs=[inside] * 4 + [anywhere] * 3,
+        out_specs=[anywhere] * 5,
+        scratch_shapes=[
+            pltpu.VMEM(block, jnp.bfloat16), pltpu.VMEM(block, jnp.bfloat16),
+            dma((2, ne)), dma((2, ne)), dma((3, ne)), dma((3, ne)),
+            dma((2, nd, ne)), dma((2, nd, ne)), dma((5,)),
+        ],
+        compiler_params=pltpu.CompilerParams(
+            collective_id=2, has_side_effects=True, vmem_limit_bytes=VMEM_BYTES
+        ),
+    )(*args)
 
 
 def combine_kernel(
@@ -239,8 +397,7 @@
 
 def fused_combine_kernel(
     ne, nd,
-    rows, grads, gate, up, down, gate_grad, up_grad, hidden, gate_turned, up_turned, hidden_turned,
-    slots, scale,
+    rows, grads, gate, up, down, ids, scale,
     mixed_out, token_out, gate_out, up_out, down_out,
     rows_in, grads_in, gate_in, up_in, down_in, gate_grad_in, up_grad_in, hidden_in,
     gate_turned_in, up_turned_in, hidden_turned_in,
@@ -285,10 +442,7 @@
     loads = [
         pltpu.make_async_copy(src, dst, load_sem.at[at])
         for at, (src, dst) in enumerate((
-            (gate_turned, gate_turned_in), (rows, rows_in), (up_turned, up_turned_in),
-            (hidden_turned, hidden_turned_in), (grads, grads_in),
-            (hidden, hidden_in), (down, down_in), (gate_grad, gate_grad_in), (gate, gate_in),
-            (up_grad, up_grad_in), (up, up_in),
+            (gate, gate_in), (up, up_in), (down, down_in), (rows, rows_in), (grads, grads_in),
         ))
     ]
     for load in loads:
@@ -297,8 +451,32 @@
     for load in loads:
         load.wait()
 
-    def dot(left, right):
-        return jnp.dot(left, right, preferred_element_type=jnp.float32)
+    width = gate_in.shape[0]
+    identity = jnp.where(
+        lax.broadcasted_iota(jnp.int32, (width, width), 0)
+        == lax.broadcasted_iota(jnp.int32, (width, width), 1), 1.0, 0.0
+    ).astype(jnp.bfloat16)
+
+    @pl.loop(0, rows_in.shape[0] // 256)
+    def _(tile):
+        lines = columns_of(tile, 256)
+        rows_now = rows_in[lines, :]
+        pre_gate = dot_turned(rows_now, gate_in[...])
+        pre_up = dot_turned(rows_now, up_in[...])
+        hidden_grad = dot_turned(grads_in[lines, :], down_in[...])
+        squash = jax.nn.sigmoid(pre_gate)
+        hidden = (pre_gate * squash * pre_up).astype(jnp.bfloat16)
+        gate_grad = (
+            hidden_grad * pre_up * (squash * (1.0 + pre_gate * (1.0 - squash)))
+        ).astype(jnp.bfloat16)
+        up_grad = (hidden_grad * (pre_gate * squash)).astype(jnp.bfloat16)
+        for value, plain, turned in (
+            (hidden, hidden_in, hidden_turned_in),
+            (gate_grad, gate_grad_in, gate_turned_in),
+            (up_grad, up_grad_in, up_turned_in),
+        ):
+            plain[lines, :] = value
+            turned[:, lines] = dot_turned(identity, value).astype(jnp.bfloat16)
 
     def make_weights(s):
         columns = columns_of(peer(s), depth)
@@ -379,10 +557,20 @@
         for k in range(2):
             home_copy(k, s, source(s)).wait()
 
-    tok_rows = slots.shape[0]
-    places = lax.broadcasted_iota(jnp.int32, (tok_rows, block), 1)
+    tok_rows = ids.shape[0]
+    experts = lax.broadcasted_iota(jnp.int32, (tok_rows, 128), 1)
+    named = [jnp.where(experts == ids[:, k : k + 1], 1.0, 0.0) for k in range(TOPK)]
+    earlier = jnp.where(
+        lax.broadcasted_iota(jnp.int32, (tok_rows, tok_rows), 0)
+        > lax.broadcasted_iota(jnp.int32, (tok_rows, tok_rows), 1), 1.0, 0.0
+    ).astype(jnp.bfloat16)
+    place = dot(earlier, (named[0] + named[1]).astype(jnp.bfloat16)) + (experts * cap).astype(
+        jnp.float32
+    )
+    places = lax.broadcasted_iota(jnp.int32, (tok_rows, block), 1).astype(jnp.float32)
     chosen = [
-        jnp.where(places == slots[:, k : k + 1], 1.0, 0.0).astype(jnp.float32) for k in range(TOPK)
+        jnp.where(places == jnp.sum(one * place, axis=1, keepdims=True), 1.0, 0.0)
+        for one in named
     ]
     either = (chosen[0] + chosen[1]).astype(jnp.bfloat16)
     first, second = (one.astype(jnp.bfloat16) for one in chosen)
@@ -409,25 +597,28 @@
 
 
 def fused_combine(ne, nd, capacity, args, weight_type):
-    rows, gate, turned, slots = args[0], args[2], args[8], args[11]
-    features = rows.shape[1]
+    rows, gate, ids = args[0], args[2], args[5]
+    total, features = rows.shape
+    width = gate.shape[0]
     anywhere, inside = pl.BlockSpec(memory_space=pl.ANY), pl.BlockSpec(memory_space=pltpu.VMEM)
-    token_type = jax.ShapeDtypeStruct((slots.shape[0], features), jnp.bfloat16)
+    token_type = jax.ShapeDtypeStruct((ids.shape[0], features), jnp.bfloat16)
     dma = pltpu.SemaphoreType.DMA
     block = (ne, capacity, features)
     return pl.pallas_call(
         functools.partial(fused_combine_kernel, ne, nd),
         out_shape=[token_type] * 2 + [weight_type] * 3,
-        in_specs=[anywhere] * 11 + [inside] * 2,
+        in_specs=[anywhere] * 5 + [inside] * 2,
         out_specs=[inside] * 2 + [anywhere] * 3,
-        scratch_shapes=[pltpu.VMEM(part.shape, part.dtype) for part in args[:11]] + [
+        scratch_shapes=[pltpu.VMEM(part.shape, part.dtype) for part in args[:5]] + [
+            *([pltpu.VMEM((total, width), jnp.bfloat16)] * 3),
+            *([pltpu.VMEM((width, total), jnp.bfloat16)] * 3),
             pltpu.VMEM((3,) + weight_type.shape, jnp.bfloat16),
             pltpu.VMEM((2, nd) + block, jnp.bfloat16),
             pltpu.VMEM((2, nd - 1) + block, jnp.bfloat16),
             pltpu.VMEM((2,) + block, jnp.bfloat16),
             pltpu.VMEM((2,) + block, jnp.bfloat16),
             dma((2, ne)), dma((2, ne)), dma((3, ne)), dma((3, ne)),
-            dma((2, nd, ne)), dma((2, nd, ne)), dma((11,)), dma((3,)),
+            dma((2, nd, ne)), dma((2, nd, ne)), dma((5,)), dma((3,)),
         ],
         compiler_params=pltpu.CompilerParams(
             collective_id=1, has_side_effects=True, vmem_limit_bytes=VMEM_BYTES
@@ -454,9 +645,25 @@
     tok_rows, features = tokens.shape
     pair_count = tok_rows * TOPK
     capacity = max(2, 5 * pair_count // (4 * experts))
+    slots = experts * capacity
+    if depth % 256 == 0 and capacity % 8 == 0 and width % 16 == 0 and nd * slots % 256 == 0:
+        weights = tuple(part.transpose(0, 2, 1) for part in (gate_weight, up_weight, down_weight))
+        rows, grads, *landed = fused_dispatch(
+            ne, nd, capacity,
+            (tokens, cotangent, expert_ids.T, gate_prob) + weights,
+            jax.ShapeDtypeStruct((nd, experts, capacity, features), jnp.bfloat16),
+            jax.ShapeDtypeStruct((width, features), jnp.bfloat16),
+        )
+        total = nd * slots
+        mixed_out, grad_tokens, *weight_grads = fused_combine(
+            ne, nd, capacity,
+            (rows.reshape(total, features), grads.reshape(total, features), *landed,
+             expert_ids, gate_prob),
+            jax.ShapeDtypeStruct(weights[0].shape, jnp.bfloat16),
+        )
+        return (mixed_out, grad_tokens, *(part.transpose(0, 2, 1) for part in weight_grads))
     slot_of = slot_index(expert_ids, experts, capacity)
     gate_scale = gate_prob.reshape(-1)
-    slots = experts * capacity
     send_rows = (
         jnp.zeros((slots, features), jnp.bfloat16).at[slot_of].set(jnp.repeat(tokens, TOPK, axis=0))
     )
@@ -468,56 +675,41 @@
     dma = pltpu.SemaphoreType.DMA
     pair_type = jax.ShapeDtypeStruct((nd,) + slot_shape, jnp.bfloat16)
     home_type = jax.ShapeDtypeStruct(slot_shape, jnp.bfloat16)
-    aligned = depth % 256 == 0 and capacity % 8 == 0 and width % 16 == 0
-    weights = (gate_weight, up_weight, down_weight)
-    if aligned:
-        weights = tuple(part.transpose(0, 2, 1) for part in weights)
-        landed_type = jax.ShapeDtypeStruct((width, features), jnp.bfloat16)
-    else:
-        landed_type = jax.ShapeDtypeStruct(gate_weight.shape, jnp.bfloat16)
-    weight_type = jax.ShapeDtypeStruct(weights[0].shape, jnp.bfloat16)
+    weight_type = jax.ShapeDtypeStruct(gate_weight.shape, jnp.bfloat16)
     rows, grads, gate, up, down = comm_call(
         dispatch_kernel, ne, nd,
-        (send_rows.reshape(slot_shape), send_grads.reshape(slot_shape)) + weights,
-        [pair_type] * 2 + [landed_type] * 3,
+        (send_rows.reshape(slot_shape), send_grads.reshape(slot_shape),
+         gate_weight, up_weight, down_weight),
+        [pair_type] * 2 + [weight_type] * 3,
         [dma((2, ne)), dma((2, ne)), dma((3, ne)), dma((3, ne)),
          dma((2, nd, ne)), dma((2, nd, ne)), dma((5,))],
         0,
     )
     total = nd * slots
     rows, grads = rows.reshape(total, features), grads.reshape(total, features)
-    if not aligned:
-        gate, up, down = (part.reshape(features, width) for part in (gate, up, down))
+    gate, up, down = (part.reshape(features, width) for part in (gate, up, down))
     contracted = (((0,), (0,)), ((), ()))
     turned = (((1,), (1,)), ((), ()))
 
-    def dot(left, right, dims):
+    def dot_by(left, right, dims):
         return lax.dot_general(left, right, dims, preferred_element_type=jnp.float32)
 
-    ahead = turned if aligned else (((1,), (0,)), ((), ()))
-    pre_gate = dot(rows, gate, ahead)
-    pre_up = dot(rows, up, ahead)
-    hidden_grad = dot(grads, down, ahead)
+    ahead = (((1,), (0,)), ((), ()))
+    pre_gate = dot_by(rows, gate, ahead)
+    pre_up = dot_by(rows, up, ahead)
+    hidden_grad = dot_by(grads, down, ahead)
     squash = jax.nn.sigmoid(pre_gate)
     hidden = (pre_gate * squash * pre_up).astype(jnp.bfloat16)
     gate_grad = (hidden_grad * pre_up * (squash * (1.0 + pre_gate * (1.0 - squash)))).astype(
         jnp.bfloat16
     )
     up_grad = (hidden_grad * (pre_gate * squash)).astype(jnp.bfloat16)
-    if aligned:
-        mixed_out, grad_tokens, *weight_grads = fused_combine(
-            ne, nd, capacity,
-            (rows, grads, gate, up, down, gate_grad, up_grad, hidden,
-             gate_grad.T, up_grad.T, hidden.T, slot_of.reshape(tok_rows, TOPK), gate_prob),
-            weight_type,
-        )
-        return (mixed_out, grad_tokens, *(part.transpose(0, 2, 1) for part in weight_grads))
     totals = tuple(
-        dot(left, right, contracted).astype(jnp.bfloat16).reshape(gate_weight.shape)
+        dot_by(left, right, contracted).astype(jnp.bfloat16).reshape(gate_weight.shape)
         for left, right in ((rows, gate_grad), (rows, up_grad), (grads, hidden))
     )
-    outputs = dot(hidden, down, turned).astype(jnp.bfloat16)
-    input_grads = (dot(gate_grad, gate, turned) + dot(up_grad, up, turned)).astype(jnp.bfloat16)
+    outputs = dot_by(hidden, down, turned).astype(jnp.bfloat16)
+    input_grads = (dot_by(gate_grad, gate, turned) + dot_by(up_grad, up, turned)).astype(jnp.bfloat16)
     out_home, in_home, grad_gate, grad_up, grad_down = comm_call(
         combine_kernel, ne, nd,
         (outputs.reshape((nd,) + slot_shape), input_grads.reshape((nd,) + slot_shape)) + totals,

time: 375 us -> 377 us (level)
  Pallas kernels: 320 us -> 364 us
  local copies, waits for them, and re-layouts: 29.9 us -> 11.6 us
  other arithmetic: 13.4 us -> 0 us
  matrix products: 10.5 us -> 0 us
    pallas_call x1, Pallas kernels: 164 us -> 206 us  [fused_combine(): pl.pallas_call(functools.partial(fused_combine_kernel, ne, nd), out_shape...]
    dot_general x3 -> x0, matrix products: 10.5 us -> none  [dot(): lax.dot_general(left, right, dims, preferred_element_type=jnp.float32)]
    dot_general x3 -> x0, local copies, waits for them, and re-layouts: 8.49 us -> none  [dot(): lax.dot_general(left, right, dims, preferred_element_type=jnp.float32)]
    convert_element_type x3 -> x0, other arithmetic: 7.66 us -> none  [the longest x2 7.65 us: shards(): hidden = (pre_gate * squash * pre_up).astype(jnp.bfloat16)]
    scatter x1 -> x0, other arithmetic: 4.39 us -> none  [shards(): jnp.zeros((slots, features), jnp.bfloat16).at[slot_of].set(scaled)]
    unnamed x33 -> x13, local copies, waits for them, and re-layouts: 9.69 us -> 11.6 us
where the time goes in v3:
time: 377 us
  Pallas kernels  364 us (97%)
  local copies, waits for them, and re-layouts  11.6 us (3%)
    pallas_call x1, Pallas kernels, fused_combine(): pl.pallas_call(functools.partial(fused_combine_kernel, ne, nd), out_shape...  206 us
    pallas_call x1, Pallas kernels, fused_dispatch(): pl.pallas_call(functools.partial(fused_dispatch_kernel, ne, nd), out_shap...  159 us
    unnamed x13, local copies, waits for them, and re-layouts  11.6 us

profile of v3, /device:TPU:9, one launch (start us, length us, event | category | flops | bytes accessed | tf_op | source)
XLA Modules:
  0.0 376.5 jit_solution(9121157867239927502)
XLA Ops:
  0.6 1.4 copy.12.scale
  2.0 1.4 copy.13.ids
  3.5 158.7 %shard_map.110 = (bf16[4,8,40,2048]{3,2,1,0:T(8,128)(2,1)}, bf16[4,8,40,2048]{3,2,1,0:T(8,128)(2,1)}, bf16[352,2048]{1,0:T(8,128)(2,1)}, bf16[352,2048]{1,0:T(8,128)(2,1)}, bf16[352,2048]{1,0:T(8,128)(2,1)}) custom-call(bf16[128,2048]{1,0:T(8,128)(2,1)} %tokens.1, bf16[128,2048]{1,0:T(8,128)(2,1)} %cotangent.1, s32[2,128]{1,0:T(2,128)} %bitcast.17, ...), custom_call_target="tpu_custom_call" | custom-call | tf_op jit(solution)/shard_map/pallas_call | solution.py:277
  162.1 205.6 %shard_map.111 = (bf16[128,2048]{1,0:T(8,128)(2,1)}, bf16[128,2048]{1,0:T(8,128)(2,1)}, bf16[8,352,256]{2,1,0:T(8,128)(2,1)}, bf16[8,352,256]{2,1,0:T(8,128)(2,1)}, bf16[8,352,256]{2,1,0:T(8,128)(2,1)}) custom-call(bf16[1280,2048]{1,0:T(8,128)(2,1)} %bitcast.9, bf16[1280,2048]{1,0:T(8,128)(2,1)} %bitcast.10, bf16[352,2048]{1,0:T(8,128)(2,1)} %get-tuple-element.17.gate, ...), custom_call_target="tpu_custom_call" | custom-call | tf_op jit(solution)/shard_map/pallas_call | solution.py:607
  367.8 0.0 copy-start.2
  367.8 2.0 copy.20
  369.8 1.9 copy.21
  371.6 0.0 copy-done.2
  371.6 0.0 copy-start.1
  371.6 1.1 copy.22
  372.8 0.8 copy-done.1
  373.5 0.0 copy-start
  373.5 1.1 copy.23
  374.6 0.8 copy-done
  375.4 1.1 copy.24
Async XLA Ops:
  367.8 3.9 %copy-start.2 = (bf16[8,352,256]{2,1,0:T(8,128)(2,1)S(1)}, bf16[8,352,256]{2,1,0:T(8,128)(2,1)}, u32[]{:S(2)}) copy-start(bf16[8,352,256]{2,1,0:T(8,128)(2,1)} %get-tuple-element.22) | copy-start | bytes 4325380
  371.6 1.9 copy-start.1
  373.5 1.9 copy-start

commit v4 on v3

--- a/solution.py
+++ b/solution.py
@@ -397,7 +397,8 @@
 
 def fused_combine_kernel(
     ne, nd,
-    rows, grads, gate, up, down, ids, scale,
+    rows, grads, gate, up, down, gate_grad, up_grad, hidden, gate_turned, up_turned, hidden_turned,
+    ids, scale,
     mixed_out, token_out, gate_out, up_out, down_out,
     rows_in, grads_in, gate_in, up_in, down_in, gate_grad_in, up_grad_in, hidden_in,
     gate_turned_in, up_turned_in, hidden_turned_in,
@@ -442,7 +443,10 @@
     loads = [
         pltpu.make_async_copy(src, dst, load_sem.at[at])
         for at, (src, dst) in enumerate((
-            (gate, gate_in), (up, up_in), (down, down_in), (rows, rows_in), (grads, grads_in),
+            (gate_turned, gate_turned_in), (rows, rows_in), (up_turned, up_turned_in),
+            (hidden_turned, hidden_turned_in), (grads, grads_in),
+            (hidden, hidden_in), (down, down_in), (gate_grad, gate_grad_in), (gate, gate_in),
+            (up_grad, up_grad_in), (up, up_in),
         ))
     ]
     for load in loads:
@@ -450,33 +454,6 @@
     greet(ne, nd)
     for load in loads:
         load.wait()
-
-    width = gate_in.shape[0]
-    identity = jnp.where(
-        lax.broadcasted_iota(jnp.int32, (width, width), 0)
-        == lax.broadcasted_iota(jnp.int32, (width, width), 1), 1.0, 0.0
-    ).astype(jnp.bfloat16)
-
-    @pl.loop(0, rows_in.shape[0] // 256)
-    def _(tile):
-        lines = columns_of(tile, 256)
-        rows_now = rows_in[lines, :]
-        pre_gate = dot_turned(rows_now, gate_in[...])
-        pre_up = dot_turned(rows_now, up_in[...])
-        hidden_grad = dot_turned(grads_in[lines, :], down_in[...])
-        squash = jax.nn.sigmoid(pre_gate)
-        hidden = (pre_gate * squash * pre_up).astype(jnp.bfloat16)
-        gate_grad = (
-            hidden_grad * pre_up * (squash * (1.0 + pre_gate * (1.0 - squash)))
-        ).astype(jnp.bfloat16)
-        up_grad = (hidden_grad * (pre_gate * squash)).astype(jnp.bfloat16)
-        for value, plain, turned in (
-            (hidden, hidden_in, hidden_turned_in),
-            (gate_grad, gate_grad_in, gate_turned_in),
-            (up_grad, up_grad_in, up_turned_in),
-        ):
-            plain[lines, :] = value
-            turned[:, lines] = dot_turned(identity, value).astype(jnp.bfloat16)
 
     def make_weights(s):
         columns = columns_of(peer(s), depth)
@@ -597,9 +574,8 @@
 
 
 def fused_combine(ne, nd, capacity, args, weight_type):
-    rows, gate, ids = args[0], args[2], args[5]
-    total, features = rows.shape
-    width = gate.shape[0]
+    rows, ids = args[0], args[11]
+    features = rows.shape[1]
     anywhere, inside = pl.BlockSpec(memory_space=pl.ANY), pl.BlockSpec(memory_space=pltpu.VMEM)
     token_type = jax.ShapeDtypeStruct((ids.shape[0], features), jnp.bfloat16)
     dma = pltpu.SemaphoreType.DMA
@@ -607,18 +583,16 @@
     return pl.pallas_call(
         functools.partial(fused_combine_kernel, ne, nd),
         out_shape=[token_type] * 2 + [weight_type] * 3,
-        in_specs=[anywhere] * 5 + [inside] * 2,
+        in_specs=[anywhere] * 11 + [inside] * 2,
         out_specs=[inside] * 2 + [anywhere] * 3,
-        scratch_shapes=[pltpu.VMEM(part.shape, part.dtype) for part in args[:5]] + [
-            *([pltpu.VMEM((total, width), jnp.bfloat16)] * 3),
-            *([pltpu.VMEM((width, total), jnp.bfloat16)] * 3),
+        scratch_shapes=[pltpu.VMEM(part.shape, part.dtype) for part in args[:11]] + [
             pltpu.VMEM((3,) + weight_type.shape, jnp.bfloat16),
             pltpu.VMEM((2, nd) + block, jnp.bfloat16),
             pltpu.VMEM((2, nd - 1) + block, jnp.bfloat16),
             pltpu.VMEM((2,) + block, jnp.bfloat16),
             pltpu.VMEM((2,) + block, jnp.bfloat16),
             dma((2, ne)), dma((2, ne)), dma((3, ne)), dma((3, ne)),
-            dma((2, nd, ne)), dma((2, nd, ne)), dma((5,)), dma((3,)),
+            dma((2, nd, ne)), dma((2, nd, ne)), dma((11,)), dma((3,)),
         ],
         compiler_params=pltpu.CompilerParams(
             collective_id=1, has_side_effects=True, vmem_limit_bytes=VMEM_BYTES
@@ -655,10 +629,21 @@
             jax.ShapeDtypeStruct((width, features), jnp.bfloat16),
         )
         total = nd * slots
+        rows, grads = rows.reshape(total, features), grads.reshape(total, features)
+        gate, up, down = landed
+        pre_gate = dot_turned(rows, gate)
+        pre_up = dot_turned(rows, up)
+        hidden_grad = dot_turned(grads, down)
+        squash = jax.nn.sigmoid(pre_gate)
+        hidden = (pre_gate * squash * pre_up).astype(jnp.bfloat16)
+        gate_grad = (
+            hidden_grad * pre_up * (squash * (1.0 + pre_gate * (1.0 - squash)))
+        ).astype(jnp.bfloat16)
+        up_grad = (hidden_grad * (pre_gate * squash)).astype(jnp.bfloat16)
         mixed_out, grad_tokens, *weight_grads = fused_combine(
             ne, nd, capacity,
-            (rows.reshape(total, features), grads.reshape(total, features), *landed,
-             expert_ids, gate_prob),
+            (rows, grads, gate, up, down, gate_grad, up_grad, hidden,
+             gate_grad.T, up_grad.T, hidden.T, expert_ids, gate_prob),
             jax.ShapeDtypeStruct(weights[0].shape, jnp.bfloat16),
         )
         return (mixed_out, grad_tokens, *(part.transpose(0, 2, 1) for part in weight_grads))

time: 377 us -> 395 us (1.048)
  matrix products: 0 us -> 10.5 us
  local copies, waits for them, and re-layouts: 11.6 us -> 20.6 us
  Pallas kernels: 364 us -> 355 us
  other arithmetic: 0 us -> 7.69 us
    dot_general x0 -> x3, matrix products: none -> 10.5 us  [dot_turned(): lax.dot_general(left, right, (((1,), (1,)), ((), ())), preferred_element_...]
    pallas_call x1, Pallas kernels: 206 us -> 196 us  [fused_combine(): pl.pallas_call(functools.partial(fused_combine_kernel, ne, nd), out_shape...]
    convert_element_type x0 -> x2, other arithmetic: none -> 7.69 us  [shards(): hidden = (pre_gate * squash * pre_up).astype(jnp.bfloat16)]
    dot_general x0 -> x3, local copies, waits for them, and re-layouts: none -> 7.51 us  [dot_turned(): lax.dot_general(left, right, (((1,), (1,)), ((), ())), preferred_element_...]
    unnamed x13 -> x31, local copies, waits for them, and re-layouts: 11.6 us -> 10.3 us
where the time goes in v4:
time: 395 us
  Pallas kernels  355 us (90%)
  local copies, waits for them, and re-layouts  20.6 us (5%)
  matrix products  10.5 us (3%)
  other arithmetic  7.69 us (2%)
    pallas_call x1, Pallas kernels, fused_combine(): pl.pallas_call(functools.partial(fused_combine_kernel, ne, nd), out_shape...  196 us
    pallas_call x1, Pallas kernels, fused_dispatch(): pl.pallas_call(functools.partial(fused_dispatch_kernel, ne, nd), out_shap...  159 us
    dot_general x3, matrix products, dot_turned(): lax.dot_general(left, right, (((1,), (1,)), ((), ())), preferred_element_...  10.5 us
    unnamed x31, local copies, waits for them, and re-layouts  10.3 us

profile of v4, /device:TPU:9, one launch (start us, length us, event | category | flops | bytes accessed | tf_op | source)
XLA Modules:
  0.0 394.6 jit_solution(14960863138142155890)
XLA Ops:
  0.6 1.4 copy.22.scale
  2.0 158.7 %shard_map.110 = (bf16[4,8,40,2048]{3,2,1,0:T(8,128)(2,1)}, bf16[4,8,40,2048]{3,2,1,0:T(8,128)(2,1)}, bf16[352,2048]{1,0:T(8,128)(2,1)}, bf16[352,2048]{1,0:T(8,128)(2,1)}, bf16[352,2048]{1,0:T(8,128)(2,1)}) custom-call(bf16[128,2048]{1,0:T(8,128)(2,1)} %tokens.1, bf16[128,2048]{1,0:T(8,128)(2,1)} %cotangent.1, s32[2,128]{1,0:T(2,128)} %bitcast.66, ...), custom_call_target="tpu_custom_call" | custom-call | tf_op jit(solution)/shard_map/pallas_call | solution.py:277
  160.7 0.0 slice-start
  160.7 5.1 %fusion.11 = f32[1280,352]{0,1:T(8,128)S(1)} fusion(bf16[1280,2048]{1,0:T(8,128)(2,1)} %bitcast.53, bf16[352,2048]{1,0:T(8,128)(2,1)} %get-tuple-element.18.up), kind=kOutput, calls=%fused_computation.21 | convolution fusion | flops 1845493760 | bytes 8486912 | tf_op jit(solution)/shard_map/dot_general | solution.py:47
  165.9 0.0 slice-start.1
  165.9 0.0 copy-done.3
  165.9 0.0 copy-done.8
  165.9 0.0 copy-start.7
  165.9 3.3 fusion.10
  169.3 2.1 fusion.12
  171.4 2.6 fusion.8
  173.9 1.9 copy.27
  175.8 2.8 copy.25
  178.6 2.8 copy.28
  181.5 2.8 copy.23
  184.3 5.1 %multiply_convert_fusion = (bf16[1280,352]{1,0:T(8,128)(2,1)}, bf16[1280,352]{1,0:T(8,128)(2,1)}, bf16[1280,352]{1,0:T(8,128)(2,1)}) fusion(f32[1280,352]{1,0:T(8,128)} %copy.28, f32[1280,352]{1,0:T(8,128)} %copy.23, f32[1280,352]{1,0:T(8,128)} %copy.25, f32[1280,352]{1,0:T(8,128)S(1)} %copy.27), kind=kLoop, calls=%fused_computation | loop fusion | flops 6307840 | bytes 9912320 | tf_op jit(solution)/shard_map/convert_element_type | solution.py:638
  189.4 0.7 copy.29.ids
  190.2 196.4 %shard_map.111 = (bf16[128,2048]{1,0:T(8,128)(2,1)}, bf16[128,2048]{1,0:T(8,128)(2,1)}, bf16[8,352,256]{2,1,0:T(8,128)(2,1)}, bf16[8,352,256]{2,1,0:T(8,128)(2,1)}, bf16[8,352,256]{2,1,0:T(8,128)(2,1)}) custom-call(bf16[1280,2048]{1,0:T(8,128)(2,1)} %bitcast.54, bf16[1280,2048]{1,0:T(8,128)(2,1)} %bitcast.58, bf16[352,2048]{1,0:T(8,128)(2,1)} %get-tuple-element.17.gate, ...), custom_call_target="tpu_custom_call" | custom-call | tf_op jit(solution)/shard_map/pallas_call | solution.py:583
  386.6 2.0 copy.36
  388.6 2.0 copy.37
  390.6 1.1 copy.38
  391.7 1.1 copy.39
  392.8 0.8 copy-done.4
  393.5 1.1 copy.40
  (19 shorter events, 0.0 us)
Async XLA Ops:
  160.7 5.2 %copy-start.3 = (bf16[4,8,40,2048]{3,2,1,0:T(8,128)(2,1)S(1)}, bf16[4,8,40,2048]{3,2,1,0:T(8,128)(2,1)}, u32[]{:S(2)}) copy-start(bf16[4,8,40,2048]{3,2,1,0:T(8,128)(2,1)} %get-tuple-element.16) | copy-start | bytes 15728644
  160.7 5.2 %copy-start.8 = (bf16[352,2048]{1,0:T(8,128)(2,1)S(1)}, bf16[352,2048]{1,0:T(8,128)(2,1)}, u32[]{:S(2)}) copy-start(bf16[352,2048]{1,0:T(8,128)(2,1)} %get-tuple-element.19.down) | copy-start | bytes 4325380
  160.7 8.5 %slice-start = ((s8[5242880]{0:T(1024)(128)(4,1)}), s8[4194304]{0:T(1024)(128)(4,1)S(1)}, s32[]{:S(2)}) async-start(s8[5242880]{0:T(1024)(128)(4,1)} %bitcast.55), calls=%async_computation | async-start | bytes 8388608
  165.9 5.5 %copy-start = (f32[1280,352]{0,1:T(8,128)}, f32[1280,352]{0,1:T(8,128)S(1)}, u32[]{:S(2)}) copy-start(f32[1280,352]{0,1:T(8,128)S(1)} %fusion.11) | copy-start | bytes 5406724
  165.9 3.4 slice-start.1
  165.9 3.3 copy-start.7
  169.3 2.1 copy-start.2
  171.4 2.6 copy-start.1
  184.3 5.1 %copy-start.9 = (s32[128,2]{0,1:T(2,128)S(1)}, s32[128,2]{0,1:T(2,128)}, u32[]{:S(2)}) copy-start(s32[128,2]{0,1:T(2,128)} %param.9) | copy-start | bytes 3076
  386.6 4.0 %copy-start.6 = (bf16[8,352,256]{2,1,0:T(8,128)(2,1)S(1)}, bf16[8,352,256]{2,1,0:T(8,128)(2,1)}, u32[]{:S(2)}) copy-start(bf16[8,352,256]{2,1,0:T(8,128)(2,1)} %get-tuple-element.22) | copy-start | bytes 4325380
  388.6 3.1 copy-start.5
  391.7 1.9 copy-start.4

commit v5 on v3

--- a/solution.py
+++ b/solution.py
@@ -153,7 +153,7 @@
     pairs = ((rows, rows_out), (grads, grads_out))
     weights = ((gate, gate_out), (up, up_out), (down, down_out))
 
-    early = min(3, ne)
+    early = 1
 
     def peer(s):
         return lax.rem(me + s, ne)

time: 377 us -> 347 us (0.920)
  Pallas kernels: 364 us -> 335 us
    pallas_call x1, Pallas kernels: 206 us -> 175 us  [fused_combine(): pl.pallas_call(functools.partial(fused_combine_kernel, ne, nd), out_shape...]
where the time goes in v5:
time: 347 us
  Pallas kernels  335 us (97%)
  local copies, waits for them, and re-layouts  11.6 us (3%)
    pallas_call x1, Pallas kernels, fused_combine(): pl.pallas_call(functools.partial(fused_combine_kernel, ne, nd), out_shape...  175 us
    pallas_call x1, Pallas kernels, fused_dispatch(): pl.pallas_call(functools.partial(fused_dispatch_kernel, ne, nd), out_shap...  160 us
    unnamed x13, local copies, waits for them, and re-layouts  11.6 us

profile of v5, /device:TPU:9, one launch (start us, length us, event | category | flops | bytes accessed | tf_op | source)
XLA Modules:
  0.0 346.8 jit_solution(16515974508771128462)
XLA Ops:
  0.6 1.4 copy.12.scale
  2.0 1.4 copy.13.ids
  3.5 159.6 %shard_map.110 = (bf16[4,8,40,2048]{3,2,1,0:T(8,128)(2,1)}, bf16[4,8,40,2048]{3,2,1,0:T(8,128)(2,1)}, bf16[352,2048]{1,0:T(8,128)(2,1)}, bf16[352,2048]{1,0:T(8,128)(2,1)}, bf16[352,2048]{1,0:T(8,128)(2,1)}) custom-call(bf16[128,2048]{1,0:T(8,128)(2,1)} %tokens.1, bf16[128,2048]{1,0:T(8,128)(2,1)} %cotangent.1, s32[2,128]{1,0:T(2,128)} %bitcast.17, ...), custom_call_target="tpu_custom_call" | custom-call | tf_op jit(solution)/shard_map/pallas_call | solution.py:277
  163.0 175.0 %shard_map.111 = (bf16[128,2048]{1,0:T(8,128)(2,1)}, bf16[128,2048]{1,0:T(8,128)(2,1)}, bf16[8,352,256]{2,1,0:T(8,128)(2,1)}, bf16[8,352,256]{2,1,0:T(8,128)(2,1)}, bf16[8,352,256]{2,1,0:T(8,128)(2,1)}) custom-call(bf16[1280,2048]{1,0:T(8,128)(2,1)} %bitcast.9, bf16[1280,2048]{1,0:T(8,128)(2,1)} %bitcast.10, bf16[352,2048]{1,0:T(8,128)(2,1)} %get-tuple-element.17.gate, ...), custom_call_target="tpu_custom_call" | custom-call | tf_op jit(solution)/shard_map/pallas_call | solution.py:607
  338.0 0.0 copy-start.2
  338.1 2.0 copy.20
  340.0 1.9 copy.21
  341.9 0.0 copy-done.2
  341.9 0.0 copy-start.1
  341.9 1.1 copy.22
  343.0 0.8 copy-done.1
  343.8 0.0 copy-start
  343.8 1.1 copy.23
  344.9 0.8 copy-done
  345.7 1.1 copy.24
Async XLA Ops:
  338.0 3.9 %copy-start.2 = (bf16[8,352,256]{2,1,0:T(8,128)(2,1)S(1)}, bf16[8,352,256]{2,1,0:T(8,128)(2,1)}, u32[]{:S(2)}) copy-start(bf16[8,352,256]{2,1,0:T(8,128)(2,1)} %get-tuple-element.22) | copy-start | bytes 4325380
  341.9 1.9 copy-start.1
  343.8 1.9 copy-start
